TPU v7x, 32 devices: a whole 2x2x4 slice. The times are simulated.
32 devices in a mesh: branch: 4 (over y, core), leaf: 8 (over z, x).
Axes of the slice: x: 2, y: 2, z: 4, core: 2. Of those that a mesh axis runs over, the one named last changes fastest.
Arguments:
- values: bfloat16 [2, 16, 16384], P(None, None, ('branch', 'leaf')), may hold values from -6 to 6
- leaf_basis: bfloat16 [256, 64, 64], P(('branch', 'leaf')), may hold values from -0.75 to 0.75
- transfer: bfloat16 [448, 64, 64], P(('branch', 'leaf')), may hold values from -0.625 to 0.625
- local_coupling: bfloat16 [2, 448, 12, 64, 64], P(None, ('branch', 'leaf')), may hold values from -0.21875 to 0.21875
- coupling_source: int32 [448, 12], P(('branch', 'leaf')), may hold values from 0 to 23, as said below
- near_field: bfloat16 [2, 256, 12, 64, 64], P(None, ('branch', 'leaf')), may hold values from -0.21875 to 0.21875
- near_source: int32 [256, 12], P(('branch', 'leaf')), may hold values from 0 to 23, as said below
- upper_transfer: bfloat16 [4, 14, 64, 64], P('branch'), may hold values from -0.625 to 0.625
- upper_coupling: bfloat16 [2, 4, 14, 64, 64], P(None, 'branch'), may hold values from -0.75 to 0.75
- top_coupling: bfloat16 [2, 4, 3, 64, 64], P(None, 'branch'), may hold values from -0.4375 to 0.4375
Outputs:
- result: float32 [2, 16, 16384], P(None, None, ('branch', 'leaf'))
Inputs may be any that keep to these rules, and one draw needn't show every extreme that they name: `coupling_source`: entry of row r(l, p, t) lies in t to t + 2 * n_l, so its source is within n_l clusters of the target along the device order. `near_source`: entry of leaf t of a device lies in t to t + 16, so its source leaf is within 8 leaves of the target.
All inputs are finite; a program needn't handle non-finite values.
Results may differ from a plain program's by a relative error of at most 0.027.
Values may be sent and summed in bfloat16 or wider, within the bound.
A program may use at most 64 MiB of HBM per device.

v0:
```python
import jax
import jax.numpy as jnp
from jax import lax
from jax.sharding import PartitionSpec as P

LOG_LEAF = 3


def with_halo(cells, sides, width):
    for axis, dim in sides:
        count = lax.axis_size(axis)
        ends = count - 1
        head = lax.slice_in_dim(cells, 0, width, axis=dim)
        tail = lax.slice_in_dim(cells, cells.shape[dim] - width, cells.shape[dim], axis=dim)
        cells = jnp.concatenate(
            [
                lax.ppermute(tail, axis, [(i, (i + 1) % count) for i in range(ends)]),
                cells,
                lax.ppermute(head, axis, [((i + 1) % count, i) for i in range(ends)]),
            ],
            axis=dim,
        )
    return cells


def swapped(shard, axis, distance):
    return lax.ppermute(shard, axis, [(i, i ^ 1 << distance) for i in range(lax.axis_size(axis))])


def pick_row(table, index):
    return lax.dynamic_index_in_dim(table, index, 0, keepdims=False)


def per_device(
    values,
    leaf_basis,
    transfer,
    local_coupling,
    coupling_source,
    near_field,
    near_source,
    upper_transfer,
    upper_coupling,
    top_coupling,
):
    f32 = jnp.float32
    bf16 = jnp.bfloat16
    operators, rhs_count, width = values.shape
    leaves, leaf_size, rank = leaf_basis.shape
    value_wide = with_halo(values[None], ((("branch", "leaf"), 0),), 1)
    cells = values.reshape(operators, rhs_count, leaves, leaf_size)
    coef = jnp.einsum("grlq,lqk->lgrk", cells, leaf_basis, preferred_element_type=f32).astype(bf16)
    levels = [coef]
    begins = []
    begin = 0
    for level in range(1, LOG_LEAF + 1):
        count = leaves >> level - 1
        part = jnp.einsum(
            "cgrk,ckm->cgrm",
            levels[-1],
            transfer[begin : begin + count],
            preferred_element_type=f32,
        )
        part = part.reshape(count // 2, 2, operators, rhs_count, rank)
        levels.append((part[:, 0] + part[:, 1]).astype(bf16))
        begins.append(begin)
        begin += count
    device_root = levels[-1][0]
    stack = jnp.concatenate(levels[:-1], axis=0)
    coef_wide = with_halo(stack[None], ((("branch", "leaf"), 0),), 1)
    leaf_count = lax.axis_size("leaf")
    depth = leaf_count.bit_length() - 1
    leaf_index = lax.axis_index("leaf")
    upward = upper_transfer[0]
    offsets = [2 * leaf_count - 2 * (leaf_count >> step) for step in range(depth)]
    siblings = []
    owners = []
    current = device_root
    for step in range(depth):
        owner = offsets[step] + jnp.right_shift(leaf_index, step)
        other = swapped(current, "leaf", step)
        mine = jnp.einsum(
            "grk,km->grm", current, pick_row(upward, owner), preferred_element_type=f32
        )
        theirs = jnp.einsum(
            "grk,km->grm",
            other,
            pick_row(upward, jnp.bitwise_xor(owner, 1)),
            preferred_element_type=f32,
        )
        current = (mine + theirs).astype(bf16)
        siblings.append(other)
        owners.append(owner)
    branch_count = lax.axis_size("branch")
    branch_index = lax.axis_index("branch")
    subtree_roots = lax.all_gather(current[None], "branch", axis=0, tiled=True)
    order = (branch_index + 1 + jnp.arange(branch_count - 1, dtype=jnp.int32)) % branch_count
    others = jnp.take(subtree_roots, order, axis=0)
    down = jnp.einsum(
        "jgrm,gjkm->grk", others, top_coupling[:, 0], preferred_element_type=f32
    ).astype(bf16)
    sibling_mats = upper_coupling[:, 0]
    for step in range(depth - 1, -1, -1):
        owner = owners[step]
        coupling_here = lax.dynamic_index_in_dim(sibling_mats, owner, 1, keepdims=False)
        coupled = jnp.einsum(
            "grm,gkm->grk", siblings[step], coupling_here, preferred_element_type=f32
        )
        carried = jnp.einsum(
            "grm,km->grk", down, pick_row(upward, owner), preferred_element_type=f32
        )
        down = (coupled + carried).astype(bf16)
    parent = down[None]
    for level in range(LOG_LEAF - 1, -1, -1):
        count = leaves >> level
        start = begins[level]
        window_rows = coef_wide[:, start : start + count].reshape(
            3 * count, operators, rhs_count, rank
        )
        picked = jnp.take(window_rows, coupling_source[start : start + count], axis=0)
        coupled = jnp.einsum(
            "cjgrm,gcjkm->cgrk",
            picked,
            local_coupling[:, start : start + count],
            preferred_element_type=f32,
        )
        carried = jnp.einsum(
            "cgrm,ckm->cgrk",
            jnp.repeat(parent, 2, axis=0),
            transfer[start : start + count],
            preferred_element_type=f32,
        )
        parent = (coupled + carried).astype(bf16)
    far = jnp.einsum("lgrk,lqk->grlq", parent, leaf_basis, preferred_element_type=f32)
    spread = value_wide.reshape(3, operators, rhs_count, leaves, leaf_size)
    spread = jnp.transpose(spread, (1, 2, 0, 3, 4)).reshape(
        operators, rhs_count, 3 * leaves, leaf_size
    )
    picked_cells = jnp.take(spread, near_source, axis=2)
    near = jnp.einsum("grljq,gljpq->grlp", picked_cells, near_field, preferred_element_type=f32)
    return (far + near).reshape(operators, rhs_count, width)


def solution(mesh):
    in_specs = (
        P(None, None, ("branch", "leaf")),
        P(("branch", "leaf"), None, None),
        P(("branch", "leaf"), None, None),
        P(None, ("branch", "leaf"), None, None, None),
        P(("branch", "leaf"), None),
        P(None, ("branch", "leaf"), None, None, None),
        P(("branch", "leaf"), None),
        P("branch", None, None, None),
        P(None, "branch", None, None, None),
        P(None, "branch", None, None, None),
    )
    out_specs = P(None, None, ("branch", "leaf"))
    return jax.shard_map(
        per_device, mesh=mesh, in_specs=in_specs, out_specs=out_specs, check_vma=False
    )
```

profile of v0, /device:TPU:0, one launch (start us, length us, event | category | flops | bytes accessed | tf_op | source)
XLA Modules:
  0.0 79.4 jit_solution(2807708642600767846)
XLA Ops:
  0.0 1.0 %reshape.148 = bf16[2,16,8,64]{3,2,1,0:T(8,128)(2,1)S(1)} reshape(bf16[2,16,512]{2,1,0:T(8,128)(2,1)} %param.10) | data formatting | bytes 65536 | tf_op jit(solution)/shard_map/reshape | solution.py:51
  1.0 1.0 %convolution_convert_fusion = bf16[8,2,16,64]{3,2,1,0:T(8,128)(2,1)S(1)} fusion(bf16[8,64,64]{2,1,0:T(8,128)(2,1)} %param.11, bf16[2,16,8,64]{3,2,1,0:T(8,128)(2,1)S(1)} %reshape.148), kind=kOutput, calls=%fused_computation.17 | convolution fusion | flops 2113536 | bytes 131072 | tf_op jit(solution)/shard_map/grlq,lqk->lgrk/dot_general | solution.py:52
  2.1 1.1 %fusion.38 = f32[8,2,16,64]{3,2,1,0:T(8,128)S(1)} fusion(bf16[8,2,16,64]{3,2,1,0:T(8,128)(2,1)S(1)} %convolution_convert_fusion, bf16[14,64,64]{2,1,0:T(8,128)(2,1)} %param.12), kind=kOutput, calls=%fused_computation.56 | convolution fusion | flops 2097152 | bytes 229376 | tf_op jit(solution)/shard_map/cgrk,ckm->cgrm/dot_general | solution.py:58
  3.2 1.0 %fusion.48 = f32[4,2,16,64]{3,2,1,0:T(8,128)S(1)} fusion(bf16[4,2,16,64]{3,2,1,0:T(8,128)(2,1)S(1)} %fusion.53, bf16[14,64,64]{2,1,0:T(8,128)(2,1)} %param.12), kind=kOutput, calls=%fused_computation.68 | convolution fusion | flops 1048576 | bytes 114688 | tf_op jit(solution)/shard_map/cgrk,ckm->cgrm/dot_general | solution.py:58
  4.2 5.5 %collective-permute-start = (bf16[1,14,2,16,64]{4,3,2,1,0:T(8,128)(2,1)S(1)}, bf16[1,14,2,16,64]{4,3,2,1,0:T(8,128)(2,1)}, u32[]{:S(2)}, u32[]{:S(2)}) collective-permute-start(bf16[1,14,2,16,64]{4,3,2,1,0:T(8,128)(2,1)S(1)} %maximum_bitcast_fusion.1), channel_id=1, source_target_pairs={{0,1},{1,2},{2,3},{3,4},{4,5},{5,6},{6,7},{7,8},{8,9},{9,10},{10,1... | collective-permute-start | bytes 172040 | tf_op jit(solution)/shard_map/ppermute | solution.py:17
  9.7 1.3 %collective-permute-start.1 = (bf16[1,14,2,16,64]{4,3,2,1,0:T(8,128)(2,1)S(1)}, bf16[1,14,2,16,64]{4,3,2,1,0:T(8,128)(2,1)}, u32[]{:S(2)}, u32[]{:S(2)}) collective-permute-start(bf16[1,14,2,16,64]{4,3,2,1,0:T(8,128)(2,1)S(1)} %maximum_bitcast_fusion.1), channel_id=1, source_target_pairs={{1,0},{2,1},{3,2},{4,3},{5,4},{6,5},{7,6},{8,7},{9,8},{10,9},{11,1... | collective-permute-start | bytes 172040 | tf_op jit(solution)/shard_map/ppermute | solution.py:19
  11.0 4.6 %collective-permute-start.5 = (bf16[1,2,16,512]{3,2,1,0:T(8,128)(2,1)}, bf16[1,2,16,512]{3,2,1,0:T(8,128)(2,1)S(1)}, u32[]{:S(2)}, u32[]{:S(2)}) collective-permute-start(bf16[1,2,16,512]{3,2,1,0:T(8,128)(2,1)} %bitcast.196), channel_id=1, source_target_pairs={{0,1},{1,2},{2,3},{3,4},{4,5},{5,6},{6,7},{7,8},{8,9},{9,10},{10,1... | collective-permute-start | bytes 98312 | tf_op jit(solution)/shard_map/ppermute | solution.py:17
  15.5 1.3 %collective-permute-start.6 = (bf16[1,2,16,512]{3,2,1,0:T(8,128)(2,1)}, bf16[1,2,16,512]{3,2,1,0:T(8,128)(2,1)S(1)}, u32[]{:S(2)}, u32[]{:S(2)}) collective-permute-start(bf16[1,2,16,512]{3,2,1,0:T(8,128)(2,1)} %bitcast.197), channel_id=1, source_target_pairs={{1,0},{2,1},{3,2},{4,3},{5,4},{6,5},{7,6},{8,7},{9,8},{10,9},{11,1... | collective-permute-start | bytes 98312 | tf_op jit(solution)/shard_map/ppermute | solution.py:19
  16.8 0.9 %convolution_bitcast_fusion.1 = f32[1,2,2,16,64]{4,3,2,1,0:T(8,128)S(1)} fusion(bf16[2,2,16,64]{3,2,1,0:T(8,128)(2,1)S(1)} %fusion.74, bf16[14,64,64]{2,1,0:T(8,128)(2,1)} %param.12), kind=kOutput, calls=%fused_computation.22 | convolution fusion | flops 524288 | bytes 57344 | tf_op jit(solution)/shard_map/cgrk,ckm->cgrm/dot_general | solution.py:58
  17.7 2.7 %collective-permute-start.2 = (bf16[2,16,64]{2,1,0:T(8,128)(2,1)S(1)}, bf16[2,16,64]{2,1,0:T(8,128)(2,1)S(1)}, u32[]{:S(2)}, u32[]{:S(2)}) collective-permute-start(bf16[2,16,64]{2,1,0:T(8,128)(2,1)S(1)} %fusion.99), channel_id=1, source_target_pairs={{0,1},{1,0},{2,3},{3,2},{4,5},{5,4},{6,7},{7,6},{8,9},{9,8},{10,11... | collective-permute-start | bytes 12296 | tf_op jit(solution)/shard_map/ppermute | solution.py:27
  20.4 0.7 compare_select_fusion.3
  21.1 0.7 compare_and_fusion.3
  21.8 0.7 compare_select_fusion.2
  22.5 1.2 %compare_and_fusion.4 = pred[4,12]{1,0:T(4,128)(4,1)} fusion(s32[14,12]{1,0:T(8,128)} %param.14), kind=kLoop, calls=%fused_computation.149 | loop fusion | flops 288 | bytes 240 | tf_op jit(solution)/shard_map/jit(_take)/and | solution.py:120
  23.7 0.7 compare_select_fusion
  24.4 1.3 %compare_and_fusion = (pred[8,12]{1,0:T(8,128)(4,1)S(1)}, pred[8,12]{1,0:T(8,128)(4,1)}) fusion(s32[8,12]{1,0:T(8,128)} %param.16, s32[14,12]{1,0:T(8,128)} %param.14), kind=kLoop, calls=%fused_computation.126 | loop fusion | flops 1152 | bytes 960 | tf_op jit(solution)/shard_map/jit(_take)/and | solution.py:139
  25.7 0.1 reshape.178
  25.8 0.1 reshape.170
  25.9 0.6 pad_clamp_fusion.3
  26.5 0.1 reshape.162
  26.5 0.6 pad_clamp_fusion.4
  27.1 0.1 reshape.194
  27.2 0.8 %fusion.86 = f32[2,16,64]{2,1,0:T(8,128)S(1)} fusion(bf16[2,16,64]{2,1,0:T(8,128)(2,1)S(1)} %fusion.99, bf16[1,14,64,64]{3,2,1,0:T(8,128)(2,1)} %param.17, s32[]{:T(128)S(6)} %select_n.105), kind=kOutput, calls=%fused_computation.104 | convolution fusion | flops 262144 | bytes 28676 | tf_op jit(solution)/shard_map/grk,km->grm/dot_general | solution.py:82
  28.1 0.9 %concatenate.19 = bf16[1,2,16,8,64]{4,3,0,2,1:T(8,128)(2,1)S(1)} reshape(bf16[2,16,512]{2,1,0:T(8,128)(2,1)} %param.10) | data formatting | bytes 65536 | tf_op jit(solution)/shard_map/concatenate | solution.py:15
  29.0 0.0 collective-permute-done.2
  29.0 0.8 %fusion.20 = bf16[2,16,64]{2,1,0:T(8,128)(2,1)S(1)} fusion(f32[2,16,64]{2,1,0:T(8,128)S(1)} %fusion.86, bf16[2,16,64]{2,1,0:T(8,128)(2,1)S(1)} %collective-permute-done.2, bf16[1,14,64,64]{3,2,1,0:T(8,128)(2,1)} %param.17, s32[]{:T(128)S(6)} %select_n.106), kind=kOutput, calls=%fused_computation.33 | convolution fusion | flops 266240 | bytes 32772 | tf_op jit(solution)/shard_map/grk,km->grm/dot_general | solution.py:85
  29.9 1.4 %collective-permute-start.3 = (bf16[2,16,64]{2,1,0:T(8,128)(2,1)S(1)}, bf16[2,16,64]{2,1,0:T(8,128)(2,1)S(1)}, u32[]{:S(2)}, u32[]{:S(2)}) collective-permute-start(bf16[2,16,64]{2,1,0:T(8,128)(2,1)S(1)} %fusion.20), channel_id=1, source_target_pairs={{0,2},{1,3},{2,0},{3,1},{4,6},{5,7},{6,4},{7,5},{8,10},{9,11},{10,... | collective-permute-start | bytes 12296 | tf_op jit(solution)/shard_map/ppermute | solution.py:27
  31.2 0.8 %fusion.82 = f32[2,16,64]{2,1,0:T(8,128)S(1)} fusion(bf16[2,16,64]{2,1,0:T(8,128)(2,1)S(1)} %fusion.20, bf16[1,14,64,64]{3,2,1,0:T(8,128)(2,1)} %param.17, s32[]{:T(128)S(6)} %select_n.107), kind=kOutput, calls=%fused_computation.100 | convolution fusion | flops 262144 | bytes 28676 | tf_op jit(solution)/shard_map/grk,km->grm/dot_general | solution.py:82
  32.1 1.4 %collective-permute-done.3 = bf16[2,16,64]{2,1,0:T(8,128)(2,1)S(1)} collective-permute-done((bf16[2,16,64]{2,1,0:T(8,128)(2,1)S(1)}, bf16[2,16,64]{2,1,0:T(8,128)(2,1)S(1)}, u32[]{:S(2)}, u32[]{:S(2)}) %collective-permute-start.3) | collective-permute-done | bytes 4128 | tf_op jit(solution)/shard_map/ppermute | solution.py:27
  33.5 0.8 %fusion.22 = bf16[2,16,64]{2,1,0:T(8,128)(2,1)S(1)} fusion(f32[2,16,64]{2,1,0:T(8,128)S(1)} %fusion.82, bf16[2,16,64]{2,1,0:T(8,128)(2,1)S(1)} %collective-permute-done.3, bf16[1,14,64,64]{3,2,1,0:T(8,128)(2,1)} %param.17, s32[]{:T(128)S(6)} %select_n.108), kind=kOutput, calls=%fused_computation.35 | convolution fusion | flops 266240 | bytes 32772 | tf_op jit(solution)/shard_map/grk,km->grm/dot_general | solution.py:85
  34.3 2.4 %collective-permute-start.4 = (bf16[2,16,64]{2,1,0:T(8,128)(2,1)S(1)}, bf16[2,16,64]{2,1,0:T(8,128)(2,1)S(1)}, u32[]{:S(2)}, u32[]{:S(2)}) collective-permute-start(bf16[2,16,64]{2,1,0:T(8,128)(2,1)S(1)} %fusion.22), channel_id=1, source_target_pairs={{0,4},{1,5},{2,6},{3,7},{4,0},{5,1},{6,2},{7,3},{8,12},{9,13},{10,... | collective-permute-start | bytes 12296 | tf_op jit(solution)/shard_map/ppermute | solution.py:27
  36.8 0.8 %fusion.78 = f32[2,16,64]{2,1,0:T(8,128)S(1)} fusion(bf16[2,16,64]{2,1,0:T(8,128)(2,1)S(1)} %fusion.22, bf16[1,14,64,64]{3,2,1,0:T(8,128)(2,1)} %param.17, s32[]{:T(128)S(6)} %select_n.109), kind=kOutput, calls=%fused_computation.96 | convolution fusion | flops 262144 | bytes 28676 | tf_op jit(solution)/shard_map/grk,km->grm/dot_general | solution.py:82
  37.6 1.3 %collective-permute-done.4 = bf16[2,16,64]{2,1,0:T(8,128)(2,1)S(1)} collective-permute-done((bf16[2,16,64]{2,1,0:T(8,128)(2,1)S(1)}, bf16[2,16,64]{2,1,0:T(8,128)(2,1)S(1)}, u32[]{:S(2)}, u32[]{:S(2)}) %collective-permute-start.4) | collective-permute-done | bytes 4128 | tf_op jit(solution)/shard_map/ppermute | solution.py:27
  38.9 0.8 %fusion.24 = bf16[2,16,64]{2,1,0:T(8,128)(2,1)S(1)} fusion(f32[2,16,64]{2,1,0:T(8,128)S(1)} %fusion.78, bf16[2,16,64]{2,1,0:T(8,128)(2,1)S(1)} %collective-permute-done.4, bf16[1,14,64,64]{3,2,1,0:T(8,128)(2,1)} %param.17, s32[]{:T(128)S(6)} %select_n.112), kind=kOutput, calls=%fused_computation.37 | convolution fusion | flops 266240 | bytes 32772 | tf_op jit(solution)/shard_map/grk,km->grm/dot_general | solution.py:85
  39.7 9.3 %all-gather = bf16[8,16,64]{2,1,0:T(8,128)(2,1)S(1)} all-gather(bf16[2,16,64]{2,1,0:T(8,128)(2,1)S(1)} %fusion.24), channel_id=2, replica_groups=mesh['branch'=4,'leaf'=8] {'branch'}, dimensions={0}, use_global_device_ids=true | all-gather | bytes 20480 | tf_op jit(solution)/shard_map/all_gather | solution.py:96
  49.0 0.6 gather_fusion.3
  49.6 1.2 %fusion.26 = f32[2,16,64]{2,1,0:T(8,128)S(1)} fusion(bf16[3,2,16,64]{3,2,1,0:T(8,128)(2,1)S(1)} %gather_fusion.3, pred[3]{0:T(512)(128)(4,1)S(1)} %compare_and_fusion.2, bf16[1,14,64,64]{3,2,1,0:T(8,128)(2,1)} %param.17, s32[]{:T(128)S(6)} %select_n.109, bf16[2,1,3,64,64]{4,3,2,1,0:T(8,128)(2,1)} %param.19), kind=kOutput, calls=%fused_computation.39 | convolution fusion | flops 1056768 | bytes 135175 | tf_op jit(solution)/shard_map/grm,km->grk/dot_general | solution.py:109
  50.8 1.0 %fusion.27 = f32[2,16,64]{2,1,0:T(8,128)S(1)} fusion(f32[2,16,64]{2,1,0:T(8,128)S(1)} %fusion.26, bf16[2,16,64]{2,1,0:T(8,128)(2,1)S(1)} %collective-permute-done.4, bf16[2,1,14,64,64]{4,3,2,1,0:T(8,128)(2,1)} %param.18, s32[]{:T(128)S(6)} %select_n.109, bf16[1,14,64,64]{3,2,1,0:T(8,128)(2,1)} %param.17, s32[]{:T(128)S(6)} %select_n.107), kind=kOutput, calls=%fused_computation.40 | convolution fusion | flops 528384 | bytes 69640 | tf_op jit(solution)/shard_map/grm,km->grk/dot_general | solution.py:109
  51.8 1.0 %fusion.28 = f32[2,16,64]{2,1,0:T(8,128)S(1)} fusion(f32[2,16,64]{2,1,0:T(8,128)S(1)} %fusion.27, bf16[2,16,64]{2,1,0:T(8,128)(2,1)S(1)} %collective-permute-done.3, bf16[2,1,14,64,64]{4,3,2,1,0:T(8,128)(2,1)} %param.18, s32[]{:T(128)S(6)} %select_n.107, bf16[1,14,64,64]{3,2,1,0:T(8,128)(2,1)} %param.17, s32[]{:T(128)S(6)} %select_n.105), kind=kOutput, calls=%fused_computation.41 | convolution fusion | flops 528384 | bytes 69640 | tf_op jit(solution)/shard_map/grm,km->grk/dot_general | solution.py:109
  52.9 0.9 %fusion.19 = bf16[2,16,64]{2,1,0:T(8,128)(2,1)S(1)} fusion(f32[2,16,64]{2,1,0:T(8,128)S(1)} %fusion.28, bf16[2,16,64]{2,1,0:T(8,128)(2,1)S(1)} %collective-permute-done.2, bf16[2,1,14,64,64]{4,3,2,1,0:T(8,128)(2,1)} %param.18, s32[]{:T(128)S(6)} %select_n.105), kind=kOutput, calls=%fused_computation.32 | convolution fusion | flops 266240 | bytes 49156 | tf_op jit(solution)/shard_map/grm,gkm->grk/dot_general | solution.py:106
  53.8 0.0 collective-permute-done.5
  53.8 0.1 concatenate.18
  53.9 0.0 collective-permute-done.6
  53.9 0.1 concatenate.20
  54.0 0.1 maximum_bitcast_fusion
  54.1 1.6 %gather_fusion.4 = bf16[96,2,16,64]{3,2,1,0:T(8,128)(2,1)} fusion(bf16[2,16,24,64]{3,1,2,0:T(8,128)(2,1)S(1)} %copy.57, s32[1024]{0:T(1024)S(1)} %pad_clamp_fusion), kind=kCustom, calls=%fused_computation.4 | custom fusion | bytes 786816 | tf_op jit(solution)/shard_map/jit(_take)/gather | solution.py:139
  55.7 2.8 %fusion.7 = f32[2,16,8,64]{3,1,0,2:T(8,128)} fusion(bf16[2,8,12,64,64]{4,3,2,1,0:T(8,128)(2,1)S(1)} %copy-done, bf16[8,12,2,16,64]{4,3,2,1,0:T(8,128)(2,1)} %bitcast.188, pred[8,12]{1,0:T(8,128)(4,1)S(1)} %get-tuple-element.7), kind=kOutput, calls=%fused_computation.14 | convolution fusion | flops 25362432 | bytes 2031712 | tf_op jit(solution)/shard_map/grljq,gljpq->grlp/dot_general | solution.py:140
  58.5 0.0 collective-permute-done
  58.5 0.0 collective-permute-done.1
  58.5 1.0 %pad_maximum_fusion = bf16[3,14,2,16,64]{4,3,2,1,0:T(8,128)(2,1)S(1)} fusion(bf16[1,14,2,16,64]{4,3,2,1,0:T(8,128)(2,1)} %collective-permute-done.1, bf16[1,14,2,16,64]{4,3,2,1,0:T(8,128)(2,1)S(1)} %maximum_bitcast_fusion.1, bf16[1,14,2,16,64]{4,3,2,1,0:T(8,128)(2,1)} %collective-permute-done), kind=kLoop, calls=%fused_computation.49 | loop fusion | flops 172032 | bytes 344064 | tf_op jit(solution)/shard_map/concatenate | solution.py:15
  59.6 0.8 pad_maximum_fusion.2
  60.3 1.3 %gather_fusion.2 = bf16[24,2,16,64]{3,2,1,0:T(8,128)(2,1)} fusion(bf16[6,2,16,64]{3,2,1,0:T(8,128)(2,1)S(1)} %bitcast.189, s32[1024]{0:T(1024)S(1)} %pad_clamp_fusion.2), kind=kCustom, calls=%fused_computation.2 | custom fusion | bytes 196704 | tf_op jit(solution)/shard_map/jit(_take)/gather | solution.py:120
  61.6 1.6 %convolution_bitcast_fusion.2 = f32[2,2,16,64]{3,2,1,0:T(8,128)S(1)} fusion(bf16[2,14,12,64,64]{4,3,2,1,0:T(8,128)(2,1)} %param.13, bf16[2,12,2,16,64]{4,3,2,1,0:T(8,128)(2,1)} %bitcast.195, pred[2,12]{1,0:T(4,128)(4,1)S(1)} %compare_and_fusion.3), kind=kOutput, calls=%fused_computation.23 | convolution fusion | flops 6340608 | bytes 999448 | tf_op jit(solution)/shard_map/cjgrm,gcjkm->cgrk/dot_general | solution.py:121
  63.2 1.5 %fusion.18 = bf16[2,2,16,64]{3,2,1,0:T(8,128)(2,1)} fusion(f32[2,2,16,64]{3,2,1,0:T(8,128)S(1)} %convolution_bitcast_fusion.2, bf16[14,64,64]{2,1,0:T(8,128)(2,1)} %param.12, bf16[2,16,64]{2,1,0:T(8,128)(2,1)S(1)} %fusion.19), kind=kOutput, calls=%fused_computation.24 | convolution fusion | flops 532480 | bytes 61440 | tf_op jit(solution)/shard_map/cgrm,ckm->cgrk/dot_general | solution.py:127
  64.7 0.8 %pad_maximum_fusion.1 = bf16[3,4,2,16,64]{4,3,2,1,0:T(8,128)(2,1)S(1)} fusion(bf16[1,14,2,16,64]{4,3,2,1,0:T(8,128)(2,1)} %collective-permute-done.1, bf16[1,14,2,16,64]{4,3,2,1,0:T(8,128)(2,1)S(1)} %maximum_bitcast_fusion.1, bf16[1,14,2,16,64]{4,3,2,1,0:T(8,128)(2,1)} %collective-permute-done), kind=kLoop, calls=%fused_computation.61 | loop fusion | flops 49152 | bytes 221184 | tf_op jit(solution)/shard_map/slice | solution.py:117
  65.5 0.0 copy-start.2
  65.5 1.5 %gather_fusion.1 = bf16[48,2,16,64]{3,2,1,0:T(8,128)(2,1)} fusion(bf16[12,2,16,64]{3,2,1,0:T(8,128)(2,1)S(1)} %bitcast.187, s32[1024]{0:T(1024)} %pad_clamp_fusion.3), kind=kCustom, calls=%fused_computation.1 | custom fusion | bytes 393408 | tf_op jit(solution)/shard_map/jit(_take)/gather | solution.py:120
  67.0 2.1 %fusion.14 = f32[4,2,16,64]{3,2,1,0:T(8,128)S(1)} fusion(bf16[2,14,12,64,64]{4,3,2,1,0:T(8,128)(2,1)} %param.13, bf16[4,12,2,16,64]{4,3,2,1,0:T(8,128)(2,1)} %bitcast.192, pred[4,12]{1,0:T(4,128)(4,1)} %compare_and_fusion.4), kind=kOutput, calls=%fused_computation.18 | convolution fusion | flops 12681216 | bytes 1999360 | tf_op jit(solution)/shard_map/cjgrm,gcjkm->cgrk/dot_general | solution.py:121
  69.1 1.0 %fusion.17 = bf16[4,2,16,64]{3,2,1,0:T(8,128)(2,1)S(1)} fusion(f32[4,2,16,64]{3,2,1,0:T(8,128)S(1)} %fusion.14, bf16[4,2,16,64]{3,2,1,0:T(8,128)(2,1)S(1)} %bitcast.198, bf16[14,64,64]{2,1,0:T(8,128)(2,1)} %param.12), kind=kOutput, calls=%fused_computation.20 | convolution fusion | flops 1064960 | bytes 131072 | tf_op jit(solution)/shard_map/cgrm,ckm->cgrk/dot_general | solution.py:127
  70.1 1.7 %gather_fusion = bf16[96,2,16,64]{3,2,1,0:T(8,128)(2,1)} fusion(bf16[24,2,16,64]{3,2,1,0:T(8,128)(2,1)S(1)} %bitcast.186, s32[1024]{0:T(1024)} %pad_clamp_fusion.4), kind=kCustom, calls=%fused_computation | custom fusion | bytes 786816 | tf_op jit(solution)/shard_map/jit(_take)/gather | solution.py:120
  71.8 3.8 %fusion.10 = f32[8,2,16,64]{3,2,1,0:T(8,128)} fusion(bf16[2,14,12,64,64]{4,3,2,1,0:T(8,128)(2,1)} %param.13, bf16[8,12,2,16,64]{4,3,2,1,0:T(8,128)(2,1)} %bitcast.190, pred[8,12]{1,0:T(8,128)(4,1)S(1)} %copy-done.3), kind=kOutput, calls=%fused_computation.15 | convolution fusion | flops 25362432 | bytes 3997792 | tf_op jit(solution)/shard_map/cjgrm,gcjkm->cgrk/dot_general | solution.py:121
  75.7 2.0 %fusion.6 = f32[2,16,8,64]{3,1,0,2:T(8,128)} fusion(f32[2,16,8,64]{3,1,0,2:T(8,128)} %fusion.7, f32[8,2,16,64]{3,2,1,0:T(8,128)} %fusion.10, bf16[8,2,16,64]{3,2,1,0:T(8,128)(2,1)S(1)} %bitcast.194, bf16[8,64,64]{2,1,0:T(8,128)(2,1)} %param.11, bf16[14,64,64]{2,1,0:T(8,128)(2,1)S(1)} %copy-done.1), kind=kOutput, calls=%fused_computation.12 | convolution fusion | flops 4243456 | bytes 458752 | tf_op jit(solution)/shard_map/lgrk,lqk->grlq/dot_general | solution.py:134
  77.7 1.0 %copy.60 = f32[2,16,8,64]{3,2,1,0:T(8,128)S(1)} copy(f32[2,16,8,64]{3,1,0,2:T(8,128)} %fusion.6) | data formatting | bytes 131072 | tf_op jit(solution)/shard_map/add | solution.py:141
  78.7 0.7 reshape.159
  (20 shorter events, 0.2 us)
Async XLA Ops:
  0.0 55.7 %copy-start = (bf16[2,8,12,64,64]{4,3,2,1,0:T(8,128)(2,1)S(1)}, bf16[2,8,12,64,64]{4,3,2,1,0:T(8,128)(2,1)}, u32[]{:S(2)}) copy-start(bf16[2,8,12,64,64]{4,3,2,1,0:T(8,128)(2,1)} %param.15) | copy-start | bytes 4718596
  4.2 54.3 %collective-permute-start = (bf16[1,14,2,16,64]{4,3,2,1,0:T(8,128)(2,1)S(1)}, bf16[1,14,2,16,64]{4,3,2,1,0:T(8,128)(2,1)}, u32[]{:S(2)}, u32[]{:S(2)}) collective-permute-start(bf16[1,14,2,16,64]{4,3,2,1,0:T(8,128)(2,1)S(1)} %maximum_bitcast_fusion.1), channel_id=1, source_target_pairs={{0,1},{1,2},{2,3},{3,4},{4,5},{5,6},{6,7},{7,8},{8,9},{9,10},{10,1... | collective-permute-start | bytes 172040 | tf_op jit(solution)/shard_map/ppermute | solution.py:17
  9.7 48.8 %collective-permute-start.1 = (bf16[1,14,2,16,64]{4,3,2,1,0:T(8,128)(2,1)S(1)}, bf16[1,14,2,16,64]{4,3,2,1,0:T(8,128)(2,1)}, u32[]{:S(2)}, u32[]{:S(2)}) collective-permute-start(bf16[1,14,2,16,64]{4,3,2,1,0:T(8,128)(2,1)S(1)} %maximum_bitcast_fusion.1), channel_id=1, source_target_pairs={{1,0},{2,1},{3,2},{4,3},{5,4},{6,5},{7,6},{8,7},{9,8},{10,9},{11,1... | collective-permute-start | bytes 172040 | tf_op jit(solution)/shard_map/ppermute | solution.py:19
  11.0 42.8 %collective-permute-start.5 = (bf16[1,2,16,512]{3,2,1,0:T(8,128)(2,1)}, bf16[1,2,16,512]{3,2,1,0:T(8,128)(2,1)S(1)}, u32[]{:S(2)}, u32[]{:S(2)}) collective-permute-start(bf16[1,2,16,512]{3,2,1,0:T(8,128)(2,1)} %bitcast.196), channel_id=1, source_target_pairs={{0,1},{1,2},{2,3},{3,4},{4,5},{5,6},{6,7},{7,8},{8,9},{9,10},{10,1... | collective-permute-start | bytes 98312 | tf_op jit(solution)/shard_map/ppermute | solution.py:17
  15.5 38.4 %collective-permute-start.6 = (bf16[1,2,16,512]{3,2,1,0:T(8,128)(2,1)}, bf16[1,2,16,512]{3,2,1,0:T(8,128)(2,1)S(1)}, u32[]{:S(2)}, u32[]{:S(2)}) collective-permute-start(bf16[1,2,16,512]{3,2,1,0:T(8,128)(2,1)} %bitcast.197), channel_id=1, source_target_pairs={{1,0},{2,1},{3,2},{4,3},{5,4},{6,5},{7,6},{8,7},{9,8},{10,9},{11,1... | collective-permute-start | bytes 98312 | tf_op jit(solution)/shard_map/ppermute | solution.py:19
  17.7 11.3 %collective-permute-start.2 = (bf16[2,16,64]{2,1,0:T(8,128)(2,1)S(1)}, bf16[2,16,64]{2,1,0:T(8,128)(2,1)S(1)}, u32[]{:S(2)}, u32[]{:S(2)}) collective-permute-start(bf16[2,16,64]{2,1,0:T(8,128)(2,1)S(1)} %fusion.99), channel_id=1, source_target_pairs={{0,1},{1,0},{2,3},{3,2},{4,5},{5,4},{6,7},{7,6},{8,9},{9,8},{10,11... | collective-permute-start | bytes 12296 | tf_op jit(solution)/shard_map/ppermute | solution.py:27
  29.9 3.7 %collective-permute-start.3 = (bf16[2,16,64]{2,1,0:T(8,128)(2,1)S(1)}, bf16[2,16,64]{2,1,0:T(8,128)(2,1)S(1)}, u32[]{:S(2)}, u32[]{:S(2)}) collective-permute-start(bf16[2,16,64]{2,1,0:T(8,128)(2,1)S(1)} %fusion.20), channel_id=1, source_target_pairs={{0,2},{1,3},{2,0},{3,1},{4,6},{5,7},{6,4},{7,5},{8,10},{9,11},{10,... | collective-permute-start | bytes 12296 | tf_op jit(solution)/shard_map/ppermute | solution.py:27
  34.3 4.6 %collective-permute-start.4 = (bf16[2,16,64]{2,1,0:T(8,128)(2,1)S(1)}, bf16[2,16,64]{2,1,0:T(8,128)(2,1)S(1)}, u32[]{:S(2)}, u32[]{:S(2)}) collective-permute-start(bf16[2,16,64]{2,1,0:T(8,128)(2,1)S(1)} %fusion.22), channel_id=1, source_target_pairs={{0,4},{1,5},{2,6},{3,7},{4,0},{5,1},{6,2},{7,3},{8,12},{9,13},{10,... | collective-permute-start | bytes 12296 | tf_op jit(solution)/shard_map/ppermute | solution.py:27
  65.5 3.6 %copy-start.2 = (bf16[2,2,16,64]{3,2,1,0:T(8,128)(2,1)S(1)}, bf16[2,2,16,64]{3,2,1,0:T(8,128)(2,1)}, u32[]{:S(2)}) copy-start(bf16[2,2,16,64]{3,2,1,0:T(8,128)(2,1)} %fusion.18) | copy-start | bytes 24580
  65.5 6.3 %copy-start.3 = (pred[8,12]{1,0:T(8,128)(4,1)S(1)}, pred[8,12]{1,0:T(8,128)(4,1)}, u32[]{:S(2)}) copy-start(pred[8,12]{1,0:T(8,128)(4,1)} %get-tuple-element.8) | copy-start | bytes 292
  71.8 3.8 %copy-start.1 = (bf16[14,64,64]{2,1,0:T(8,128)(2,1)S(1)}, bf16[14,64,64]{2,1,0:T(8,128)(2,1)}, u32[]{:S(2)}) copy-start(bf16[14,64,64]{2,1,0:T(8,128)(2,1)} %param.12) | copy-start | bytes 344068
where the time goes:
time: 81 us; the launch traced here: 79.4 us
  matrix products  28 us (35%)
  starting transfers between devices  19.1 us (24%)
  local copies, waits for them, and re-layouts  10.8 us (13%)
  blocking collectives  9.29 us (11%)
  other arithmetic  9.2 us (11%)
  waiting for transfers between devices  2.73 us (3%)
    ppermute x2, starting transfers between devices, with_halo(): lax.ppermute(tail, axis, [(i, (i + 1) % count) for i in range(ends)])  10 us
    all_gather x1, blocking collectives, per_device(): subtree_roots = lax.all_gather(current[None], 'branch', axis=0, tiled=True)  9.29 us
    dot_general x3, matrix products, per_device(): jnp.einsum('cjgrm,gcjkm->cgrk', picked, local_coupling[:, start:start + c...  7.55 us
    ppermute x3, starting transfers between devices, swapped(): lax.ppermute(shard, axis, [(i, i ^ 1 << distance) for i in range(lax.axis...  6.51 us
    gather x3, local copies, waits for them, and re-layouts, per_device(): picked = jnp.take(window_rows, coupling_source[start:start + count], axis=0)  4.42 us
    dot_general x3, matrix products, per_device(): jnp.einsum('grm,km->grk', down, pick_row(upward, owner), preferred_elemen...  3.26 us
    dot_general x3, matrix products, per_device(): jnp.einsum('cgrk,ckm->cgrm', levels[-1], transfer[begin:begin + count], p...  2.93 us
    dot_general x1, matrix products, per_device(): jnp.einsum('grljq,gljpq->grlp', picked_cells, near_field, preferred_eleme...  2.8 us
  transfers between devices with their start and end apart: 7, of which 2 were waited for; matrix products, arithmetic and copies ran while one was open for 29% of the time, Pallas kernels for 0%

commit v1 on v0

v1 whole, which is shorter than its diff:
```python
import functools

import jax
import jax.numpy as jnp
from jax import lax
from jax.experimental import pallas as pl
from jax.experimental.pallas import tpu as pltpu
from jax.sharding import PartitionSpec as P

LOG_LEAF = 3
F32 = jnp.float32
BF16 = jnp.bfloat16
MESH = pl.DeviceIdType.MESH


def dot(a, b):
    return jnp.dot(a, b, preferred_element_type=F32)


def dot_nt(a, b):
    return lax.dot_general(a, b, (((1,), (1,)), ((), ())), preferred_element_type=F32)


def side_by_side(blocks):
    pairs = []
    for i in range(0, len(blocks) - 1, 2):
        pairs.append(jnp.concatenate(blocks[i : i + 2], axis=1))
    if len(blocks) % 2:
        pairs.append(blocks[-1])
    return pairs[0] if len(pairs) == 1 else jnp.concatenate(pairs, axis=1)


def kernel(
    branch_count,
    leaf_count,
    values,
    leaf_basis,
    transfer,
    local_coupling,
    near_field,
    upper_transfer,
    upper_coupling,
    top_coupling,
    coupling_source,
    near_source,
    out,
    val,
    basis,
    trans,
    couple,
    near,
    up_trans,
    up_couple,
    top,
    value_win,
    coef_win,
    upper,
    roots,
    coupled,
    near_part,
    load_sem,
    halo_send,
    halo_recv,
    leaf_send,
    leaf_recv,
    branch_send,
    branch_recv,
):
    operators, rhs_count, _ = val.shape
    cols = operators * rhs_count
    leaves, leaf_size, rank = basis.shape
    rows = trans.shape[0]
    blocks = couple.shape[2]
    near_blocks = near.shape[2]
    depth = leaf_count.bit_length() - 1
    b = lax.axis_index("branch")
    j = lax.axis_index("leaf")
    p = b * leaf_count + j
    last = branch_count * leaf_count - 1

    starts = [2 * leaves - 2 * (leaves >> level) for level in range(LOG_LEAF)]
    pieces = [
        (values, val),
        (leaf_basis, basis),
        (transfer, trans),
        (upper_transfer.at[0], up_trans),
        (near_field, near),
        (local_coupling, couple),
        (upper_coupling.at[:, 0], up_couple),
        (top_coupling.at[:, 0], top),
    ]
    loads = [
        pltpu.make_async_copy(src, dst, load_sem.at[i]) for i, (src, dst) in enumerate(pieces)
    ]
    for load in loads:
        load.start()
    val_load, basis_load, trans_load, ut_load, near_load, couple_load, uc_load, top_load = loads

    barrier = pltpu.get_barrier_semaphore()

    def greet(bb, jj):
        pl.semaphore_signal(barrier, inc=1, device_id=(bb, jj), device_id_type=MESH)

    for d in range(1, leaf_count):
        greet(b, lax.rem(j + d, leaf_count))
    for d in range(1, branch_count):
        greet(lax.rem(b + d, branch_count), j)
    low_edge = jnp.logical_and(j == 0, b > 0)
    high_edge = jnp.logical_and(j == leaf_count - 1, b < branch_count - 1)

    @pl.when(low_edge)
    def _():
        greet(b - 1, leaf_count - 1)

    @pl.when(high_edge)
    def _():
        greet(b + 1, 0)

    @pl.when(p == 0)
    def _():
        value_win[0:leaves] = jnp.zeros((leaves, cols, leaf_size), BF16)
        coef_win[0:rows] = jnp.zeros((rows, cols, rank), BF16)

    @pl.when(p == last)
    def _():
        value_win[2 * leaves :] = jnp.zeros((leaves, cols, leaf_size), BF16)
        coef_win[2 * rows :] = jnp.zeros((rows, cols, rank), BF16)

    val_load.wait()
    basis_load.wait()
    cells = val[...].reshape(cols, leaves * leaf_size)
    level = []
    for t in range(leaves):
        cell = cells[:, t * leaf_size : (t + 1) * leaf_size]
        value_win[leaves + t] = cell
        coef = dot(cell, basis[t]).astype(BF16)
        coef_win[rows + t] = coef
        level.append(coef)
    trans_load.wait()
    begin = 0
    for step in range(LOG_LEAF):
        count = leaves >> step
        above = []
        for t in range(count // 2):
            pair = side_by_side(level[2 * t : 2 * t + 2])
            mats = trans[begin + 2 * t : begin + 2 * t + 2].reshape(2 * rank, rank)
            coef = dot(pair, mats).astype(BF16)
            if step < LOG_LEAF - 1:
                coef_win[rows + begin + count + t] = coef
            above.append(coef)
        begin += count
        level = above
    upper[j] = level[0]

    greeted = leaf_count - 1 + branch_count - 1
    greeted += low_edge.astype(jnp.int32) + high_edge.astype(jnp.int32)
    pl.semaphore_wait(barrier, greeted)

    def leaf_copy(d, slot):
        return pltpu.make_async_remote_copy(
            src_ref=upper.at[slot],
            dst_ref=upper.at[slot],
            send_sem=leaf_send.at[d - 1],
            recv_sem=leaf_recv.at[d - 1],
            device_id=(b, lax.rem(j + d, leaf_count)),
            device_id_type=MESH,
        )

    for d in range(1, leaf_count):
        leaf_copy(d, j).start()

    def halo(window, size, kind, way):
        place = 0 if way == 0 else 2 * size
        other = p + 1 if way == 0 else p - 1
        return pltpu.make_async_remote_copy(
            src_ref=window.at[pl.ds(size, size)],
            dst_ref=window.at[pl.ds(place, size)],
            send_sem=halo_send.at[2 * kind + way],
            recv_sem=halo_recv.at[2 * kind + way],
            device_id=(other // leaf_count, lax.rem(other, leaf_count)),
            device_id_type=MESH,
        )

    halos = ((value_win, leaves, 0), (coef_win, rows, 1))

    @pl.when(p < last)
    def _():
        for args in halos:
            halo(*args, 0).start()

    @pl.when(p > 0)
    def _():
        for args in halos:
            halo(*args, 1).start()

    ut_load.wait()
    for d in range(1, leaf_count):
        leaf_copy(d, lax.rem(j + leaf_count - d, leaf_count)).wait_recv()
    offsets = [2 * leaf_count - 2 * (leaf_count >> step) for step in range(depth + 1)]
    for step in range(depth):
        for t in range(leaf_count >> step + 1):
            low = offsets[step] + 2 * t
            pair = side_by_side([upper[low], upper[low + 1]])
            mats = up_trans[low : low + 2].reshape(2 * rank, rank)
            upper[offsets[step + 1] + t] = dot(pair, mats).astype(BF16)

    def branch_copy(d):
        return pltpu.make_async_remote_copy(
            src_ref=upper.at[offsets[depth]],
            dst_ref=roots.at[branch_count - 1 - d],
            send_sem=branch_send.at[d - 1],
            recv_sem=branch_recv.at[d - 1],
            device_id=(lax.rem(b + d, branch_count), j),
            device_id_type=MESH,
        )

    for d in range(1, branch_count):
        branch_copy(d).start()

    first = lax.broadcasted_iota(jnp.int32, (rank, cols), 1) < rhs_count

    def pick(both):
        return jnp.where(first, both[:rank], both[rank:])

    near_load.wait()

    @pl.when(p > 0)
    def _():
        halo(value_win, leaves, 0, 0).wait_recv()
        halo(coef_win, rows, 1, 0).wait_recv()

    @pl.when(p < last)
    def _():
        halo(value_win, leaves, 0, 1).wait_recv()
        halo(coef_win, rows, 1, 1).wait_recv()

    def listed(matrices, row, count, window, source):
        wide = side_by_side(
            [matrices[:, row, m].reshape(operators * rank, rank) for m in range(count)]
        )
        picked = side_by_side([window[source(m)] for m in range(count)])
        return pick(dot_nt(wide, picked))

    def near_step(t, carry):
        near_part[t] = listed(near, t, near_blocks, value_win, lambda m: near_source[t, m])
        return carry

    lax.fori_loop(0, leaves, near_step, 0, unroll=2)
    couple_load.wait()

    for step in range(LOG_LEAF):
        count = leaves >> step
        begin = starts[step]

        def couple_step(t, carry, count=count, begin=begin, shift=LOG_LEAF - step):
            row = begin + t

            def source(m):
                s = coupling_source[row, m]
                side = jnp.right_shift(s, shift)
                return side * rows + begin + jnp.bitwise_and(s, count - 1)

            coupled[row] = listed(couple, row, blocks, coef_win, source)
            return carry

        lax.fori_loop(0, count, couple_step, 0, unroll=2)

    uc_load.wait()
    top_load.wait()
    sides = []
    for step in range(depth):
        own = jnp.right_shift(j, step)
        mats = up_couple[:, offsets[step] + own].reshape(operators * rank, rank)
        sibling = upper[offsets[step] + jnp.bitwise_xor(own, 1)]
        sides.append(pick(dot_nt(mats, sibling)))

    for d in range(1, branch_count):
        branch_copy(d).wait_recv()
    tops = side_by_side(
        [top[:, m].reshape(operators * rank, rank) for m in range(branch_count - 1)]
    )
    others = side_by_side([roots[m] for m in range(branch_count - 1)])
    down = pick(dot_nt(tops, others)).astype(BF16)
    for step in range(depth - 1, -1, -1):
        mat = up_trans[offsets[step] + jnp.right_shift(j, step)]
        down = (sides[step] + dot(mat, down)).astype(BF16)
    targets = [down]
    for step in range(LOG_LEAF - 1, -1, -1):
        below = []
        for t, parent in enumerate(targets):
            low = starts[step] + 2 * t
            mats = trans[low : low + 2].reshape(2 * rank, rank)
            both = coupled[low : low + 2].reshape(2 * rank, cols) + dot(mats, parent)
            both = both.astype(BF16)
            below += [both[:rank], both[rank:]]
        targets = below
    for t in range(0, leaves, 2):
        parts = [near_part[u] + dot(basis[u], targets[u]) for u in (t, t + 1)]
        turned = jnp.concatenate(parts, axis=0).T
        out[:, :, t * leaf_size : (t + 2) * leaf_size] = turned.reshape(
            operators, rhs_count, 2 * leaf_size
        )

    for d in range(1, leaf_count):
        leaf_copy(d, j).wait_send()
    for d in range(1, branch_count):
        branch_copy(d).wait_send()

    @pl.when(p < last)
    def _():
        for args in halos:
            halo(*args, 0).wait_send()

    @pl.when(p > 0)
    def _():
        for args in halos:
            halo(*args, 1).wait_send()


def solution(mesh):
    branch_count = mesh.shape["branch"]
    leaf_count = mesh.shape["leaf"]

    def per_device(
        values,
        leaf_basis,
        transfer,
        local_coupling,
        coupling_source,
        near_field,
        near_source,
        upper_transfer,
        upper_coupling,
        top_coupling,
    ):
        operators, rhs_count, width = values.shape
        cols = operators * rhs_count
        leaves, leaf_size, rank = leaf_basis.shape
        rows = transfer.shape[0]
        upper = upper_transfer.shape[1]
        any_spec = pl.BlockSpec(memory_space=pl.ANY)
        smem = pl.BlockSpec(memory_space=pltpu.SMEM)
        dma = pltpu.SemaphoreType.DMA
        return pl.pallas_call(
            functools.partial(kernel, branch_count, leaf_count),
            out_shape=jax.ShapeDtypeStruct(values.shape, F32),
            in_specs=[any_spec] * 8 + [smem] * 2,
            out_specs=pl.BlockSpec(memory_space=pltpu.VMEM),
            scratch_shapes=[
                pltpu.VMEM(values.shape, BF16),
                pltpu.VMEM(leaf_basis.shape, BF16),
                pltpu.VMEM(transfer.shape, BF16),
                pltpu.VMEM(local_coupling.shape, BF16),
                pltpu.VMEM(near_field.shape, BF16),
                pltpu.VMEM(upper_transfer.shape[1:], BF16),
                pltpu.VMEM((operators,) + upper_coupling.shape[2:], BF16),
                pltpu.VMEM((operators,) + top_coupling.shape[2:], BF16),
                pltpu.VMEM((3 * leaves, cols, leaf_size), BF16),
                pltpu.VMEM((3 * rows, cols, rank), BF16),
                pltpu.VMEM((upper + 1, cols, rank), BF16),
                pltpu.VMEM((branch_count - 1, cols, rank), BF16),
                pltpu.VMEM((rows, rank, cols), F32),
                pltpu.VMEM((leaves, leaf_size, cols), F32),
                dma((8,)),
                dma((4,)),
                dma((4,)),
                dma((leaf_count - 1,)),
                dma((leaf_count - 1,)),
                dma((branch_count - 1,)),
                dma((branch_count - 1,)),
            ],
            compiler_params=pltpu.CompilerParams(
                collective_id=0, has_side_effects=True, vmem_limit_bytes=64 * 1024 * 1024
            ),
        )(
            values,
            leaf_basis,
            transfer,
            local_coupling,
            near_field,
            upper_transfer,
            upper_coupling,
            top_coupling,
            coupling_source,
            near_source,
        )

    in_specs = (
        P(None, None, ("branch", "leaf")),
        P(("branch", "leaf"), None, None),
        P(("branch", "leaf"), None, None),
        P(None, ("branch", "leaf"), None, None, None),
        P(("branch", "leaf"), None),
        P(None, ("branch", "leaf"), None, None, None),
        P(("branch", "leaf"), None),
        P("branch", None, None, None),
        P(None, "branch", None, None, None),
        P(None, "branch", None, None, None),
    )
    out_specs = P(None, None, ("branch", "leaf"))
    return jax.shard_map(
        per_device, mesh=mesh, in_specs=in_specs, out_specs=out_specs, check_vma=False
    )
```

time: 81 us -> 24.1 us (0.30); the launches traced: 79.4 us -> 23.9 us
  matrix products: 28 us -> 0 us
  Pallas kernels: 0 us -> 22.4 us
  starting transfers between devices: 19.1 us -> 0 us
  local copies, waits for them, and re-layouts: 10.8 us -> 1.47 us
  blocking collectives: 9.29 us -> 0 us
  other arithmetic: 9.2 us -> 0 us
  waiting for transfers between devices: 2.73 us -> 0 us
    dot_general x21 -> x0, matrix products: 28 us -> none  [the longest x3 7.55 us: per_device(): jnp.einsum('cjgrm,gcjkm->cgrk', picked, local_coupling[:, start:start + c...]
    pallas_call x0 -> x1, Pallas kernels: none -> 22.4 us  [per_device(): pl.pallas_call(functools.partial(kernel, branch_count, leaf_count), out_s...]
    ppermute x7 -> x0, starting transfers between devices: 19.1 us -> none  [the longest x2 10 us: with_halo(): lax.ppermute(tail, axis, [(i, (i + 1) % count) for i in range(ends)])]
    all_gather x1 -> x0, blocking collectives: 9.29 us -> none  [per_device(): subtree_roots = lax.all_gather(current[None], 'branch', axis=0, tiled=True)]
    gather x5 -> x0, local copies, waits for them, and re-layouts: 6.59 us -> none  [the longest x3 4.42 us: per_device(): picked = jnp.take(window_rows, coupling_source[start:start + count], axis=0)]
    and x4 -> x0, other arithmetic: 3.17 us -> none  [the longest x2 1.87 us: per_device(): picked = jnp.take(window_rows, coupling_source[start:start + count], axis=0)]
    ppermute x7 -> x0, waiting for transfers between devices: 2.73 us -> none  [the longest x3 2.72 us: swapped(): lax.ppermute(shard, axis, [(i, i ^ 1 << distance) for i in range(lax.axis...]
    select_n x4 -> x0, other arithmetic: 2.1 us -> none  [the longest x2 1.38 us: per_device(): picked = jnp.take(window_rows, coupling_source[start:start + count], axis=0)]
  transfers between devices with their start and end apart: 7 -> 0, of which waited for: 2 -> 0; matrix products, arithmetic and copies ran while one was open for 29% -> 0% of each run, Pallas kernels for 0% -> 0%
where the time goes in v1:
time: 24.1 us; the launch traced here: 23.9 us
  Pallas kernels  22.4 us (93%)
  local copies, waits for them, and re-layouts  1.47 us (6%)
    pallas_call x1, Pallas kernels, per_device(): pl.pallas_call(functools.partial(kernel, branch_count, leaf_count), out_s...  22.4 us
    unnamed x1, local copies, waits for them, and re-layouts  1.47 us

profile of v1, /device:TPU:0, one launch (start us, length us, event | category | flops | bytes accessed | tf_op | source)
XLA Modules:
  0.0 23.9 jit_solution(7052624874240937359)
XLA Ops:
  0.0 22.4 %shard_map.100 = f32[2,16,512]{2,1,0:T(8,128)} custom-call(bf16[2,16,512]{2,1,0:T(8,128)(2,1)} %values.1, bf16[8,64,64]{2,1,0:T(8,128)(2,1)} %leaf_basis.1, bf16[14,64,64]{2,1,0:T(8,128)(2,1)} %transfer.1, bf16[2,14,12,64,64]{4,3,2,1,0:T(8,128)(2,1)} %local_coupling.1, bf16[2,8,12,64,64]{4,3,2,1,0:T(8,128)(2,1)} %near_field.1, ...), custom_call_target="tpu_custom_call" | custom-call | tf_op jit(solution)/shard_map/pallas_call | solution.py:344
  22.4 1.5 %copy.12 = f32[2,16,512]{2,1,0:T(8,128)} copy(f32[2,16,512]{2,1,0:T(8,128)} %shard_map.100) | data formatting | bytes 131072

commit v2 on v1

--- a/solution.py
+++ b/solution.py
@@ -44,6 +44,8 @@
     coupling_source,
     near_source,
     out,
+    coupling_index,
+    near_index,
     val,
     basis,
     trans,
@@ -54,7 +56,9 @@
     top,
     value_win,
     coef_win,
+    leaf_roots,
     upper,
+    own_root,
     roots,
     coupled,
     near_part,
@@ -70,6 +74,7 @@
     cols = operators * rhs_count
     leaves, leaf_size, rank = basis.shape
     rows = trans.shape[0]
+    cell_pairs, coef_pairs = leaves // 2, rows // 2
     blocks = couple.shape[2]
     near_blocks = near.shape[2]
     depth = leaf_count.bit_length() - 1
@@ -79,6 +84,13 @@
     last = branch_count * leaf_count - 1
 
     starts = [2 * leaves - 2 * (leaves >> level) for level in range(LOG_LEAF)]
+
+    def dense(coef):
+        return jnp.concatenate([coef[:rhs_count], coef[rhs_count:]], axis=1)
+
+    def undense(coef):
+        return jnp.concatenate([coef[:, :rank], coef[:, rank:]], axis=0)
+
     pieces = [
         (values, val),
         (leaf_basis, basis),
@@ -88,13 +100,15 @@
         (local_coupling, couple),
         (upper_coupling.at[:, 0], up_couple),
         (top_coupling.at[:, 0], top),
+        (near_source, near_index),
+        (coupling_source, coupling_index),
     ]
     loads = [
         pltpu.make_async_copy(src, dst, load_sem.at[i]) for i, (src, dst) in enumerate(pieces)
     ]
     for load in loads:
         load.start()
-    val_load, basis_load, trans_load, ut_load, near_load, couple_load, uc_load, top_load = loads
+    val_load, basis_load, trans_load, ut_load, near_load, couple_load, uc_load, top_load, ni_load, ci_load = loads
 
     barrier = pltpu.get_barrier_semaphore()
 
@@ -118,39 +132,36 @@
 
     @pl.when(p == 0)
     def _():
-        value_win[0:leaves] = jnp.zeros((leaves, cols, leaf_size), BF16)
-        coef_win[0:rows] = jnp.zeros((rows, cols, rank), BF16)
+        value_win[0:cell_pairs] = jnp.zeros((cell_pairs, cols, 2 * leaf_size), BF16)
+        coef_win[0:coef_pairs] = jnp.zeros((coef_pairs, cols, 2 * rank), BF16)
 
     @pl.when(p == last)
     def _():
-        value_win[2 * leaves :] = jnp.zeros((leaves, cols, leaf_size), BF16)
-        coef_win[2 * rows :] = jnp.zeros((rows, cols, rank), BF16)
+        value_win[2 * cell_pairs : 3 * cell_pairs] = jnp.zeros(
+            (cell_pairs, cols, 2 * leaf_size), BF16
+        )
+        coef_win[2 * coef_pairs : 3 * coef_pairs] = jnp.zeros((coef_pairs, cols, 2 * rank), BF16)
 
     val_load.wait()
     basis_load.wait()
     cells = val[...].reshape(cols, leaves * leaf_size)
     level = []
-    for t in range(leaves):
-        cell = cells[:, t * leaf_size : (t + 1) * leaf_size]
-        value_win[leaves + t] = cell
-        coef = dot(cell, basis[t]).astype(BF16)
-        coef_win[rows + t] = coef
-        level.append(coef)
+    for t in range(cell_pairs):
+        pair = cells[:, 2 * t * leaf_size : 2 * (t + 1) * leaf_size]
+        value_win[cell_pairs + t] = pair
+        level.append(dot(pair[:, :leaf_size], basis[2 * t]).astype(BF16))
+        level.append(dot(pair[:, leaf_size:], basis[2 * t + 1]).astype(BF16))
     trans_load.wait()
-    begin = 0
     for step in range(LOG_LEAF):
-        count = leaves >> step
         above = []
-        for t in range(count // 2):
+        for t in range(leaves >> step + 1):
+            low = starts[step] + 2 * t
             pair = side_by_side(level[2 * t : 2 * t + 2])
-            mats = trans[begin + 2 * t : begin + 2 * t + 2].reshape(2 * rank, rank)
-            coef = dot(pair, mats).astype(BF16)
-            if step < LOG_LEAF - 1:
-                coef_win[rows + begin + count + t] = coef
-            above.append(coef)
-        begin += count
+            coef_win[coef_pairs + low // 2] = pair
+            mats = trans[low : low + 2].reshape(2 * rank, rank)
+            above.append(dot(pair, mats).astype(BF16))
         level = above
-    upper[j] = level[0]
+    leaf_roots[j] = dense(level[0])
 
     greeted = leaf_count - 1 + branch_count - 1
     greeted += low_edge.astype(jnp.int32) + high_edge.astype(jnp.int32)
@@ -158,8 +169,8 @@
 
     def leaf_copy(d, slot):
         return pltpu.make_async_remote_copy(
-            src_ref=upper.at[slot],
-            dst_ref=upper.at[slot],
+            src_ref=leaf_roots.at[slot],
+            dst_ref=leaf_roots.at[slot],
             send_sem=leaf_send.at[d - 1],
             recv_sem=leaf_recv.at[d - 1],
             device_id=(b, lax.rem(j + d, leaf_count)),
@@ -181,7 +192,7 @@
             device_id_type=MESH,
         )
 
-    halos = ((value_win, leaves, 0), (coef_win, rows, 1))
+    halos = ((value_win, cell_pairs, 0), (coef_win, coef_pairs, 1))
 
     @pl.when(p < last)
     def _():
@@ -197,16 +208,23 @@
     for d in range(1, leaf_count):
         leaf_copy(d, lax.rem(j + leaf_count - d, leaf_count)).wait_recv()
     offsets = [2 * leaf_count - 2 * (leaf_count >> step) for step in range(depth + 1)]
+    level = [undense(leaf_roots[m]) for m in range(leaf_count)]
     for step in range(depth):
+        above = []
         for t in range(leaf_count >> step + 1):
             low = offsets[step] + 2 * t
-            pair = side_by_side([upper[low], upper[low + 1]])
+            pair = side_by_side(level[2 * t : 2 * t + 2])
             mats = up_trans[low : low + 2].reshape(2 * rank, rank)
-            upper[offsets[step + 1] + t] = dot(pair, mats).astype(BF16)
+            coef = dot(pair, mats).astype(BF16)
+            if step < depth - 1:
+                upper[offsets[step + 1] - leaf_count + t] = coef
+            above.append(coef)
+        level = above
+    own_root[...] = dense(level[0])
 
     def branch_copy(d):
         return pltpu.make_async_remote_copy(
-            src_ref=upper.at[offsets[depth]],
+            src_ref=own_root,
             dst_ref=roots.at[branch_count - 1 - d],
             send_sem=branch_send.at[d - 1],
             recv_sem=branch_recv.at[d - 1],
@@ -226,27 +244,44 @@
 
     @pl.when(p > 0)
     def _():
-        halo(value_win, leaves, 0, 0).wait_recv()
-        halo(coef_win, rows, 1, 0).wait_recv()
+        for args in halos:
+            halo(*args, 0).wait_recv()
 
     @pl.when(p < last)
     def _():
-        halo(value_win, leaves, 0, 1).wait_recv()
-        halo(coef_win, rows, 1, 1).wait_recv()
+        for args in halos:
+            halo(*args, 1).wait_recv()
+
+    for window, size, _ in halos:
+        for m in range(3 * size):
+            pair = window[m]
+            half = pair.shape[1] // 2
+            window[3 * size + m] = jnp.concatenate([pair[:, half:], pair[:, :half]], axis=1)
 
     def listed(matrices, row, count, window, source):
         wide = side_by_side(
             [matrices[:, row, m].reshape(operators * rank, rank) for m in range(count)]
         )
-        picked = side_by_side([window[source(m)] for m in range(count)])
-        return pick(dot_nt(wide, picked))
+        picked = []
+        for m in range(0, count, 2):
+            half = window.shape[2] // 2
+            left, right = window[source(m)], window[source(m + 1)]
+            picked.append(jnp.concatenate([left[:, :half], right[:, half:]], axis=1))
+        return pick(dot_nt(wide, jnp.concatenate(picked, axis=1)))
+
+    ni_load.wait()
 
     def near_step(t, carry):
-        near_part[t] = listed(near, t, near_blocks, value_win, lambda m: near_source[t, m])
+        def source(m):
+            s = near_index[t, m]
+            return jnp.bitwise_and(s + m, 1) * 3 * cell_pairs + jnp.right_shift(s, 1)
+
+        near_part[t] = listed(near, t, near_blocks, value_win, source)
         return carry
 
     lax.fori_loop(0, leaves, near_step, 0, unroll=2)
     couple_load.wait()
+    ci_load.wait()
 
     for step in range(LOG_LEAF):
         count = leaves >> step
@@ -256,9 +291,11 @@
             row = begin + t
 
             def source(m):
-                s = coupling_source[row, m]
+                s = coupling_index[row, m]
                 side = jnp.right_shift(s, shift)
-                return side * rows + begin + jnp.bitwise_and(s, count - 1)
+                place = jnp.right_shift(jnp.bitwise_and(s, count - 1), 1)
+                turned = jnp.bitwise_and(s + m, 1) * 3 * coef_pairs
+                return turned + side * coef_pairs + begin // 2 + place
 
             coupled[row] = listed(couple, row, blocks, coef_win, source)
             return carry
@@ -271,7 +308,11 @@
     for step in range(depth):
         own = jnp.right_shift(j, step)
         mats = up_couple[:, offsets[step] + own].reshape(operators * rank, rank)
-        sibling = upper[offsets[step] + jnp.bitwise_xor(own, 1)]
+        sibling = jnp.bitwise_xor(own, 1)
+        if step == 0:
+            sibling = undense(leaf_roots[sibling])
+        else:
+            sibling = upper[offsets[step] - leaf_count + sibling]
         sides.append(pick(dot_nt(mats, sibling)))
 
     for d in range(1, branch_count):
@@ -279,7 +320,7 @@
     tops = side_by_side(
         [top[:, m].reshape(operators * rank, rank) for m in range(branch_count - 1)]
     )
-    others = side_by_side([roots[m] for m in range(branch_count - 1)])
+    others = side_by_side([undense(roots[m]) for m in range(branch_count - 1)])
     down = pick(dot_nt(tops, others)).astype(BF16)
     for step in range(depth - 1, -1, -1):
         mat = up_trans[offsets[step] + jnp.right_shift(j, step)]
@@ -339,14 +380,19 @@
         rows = transfer.shape[0]
         upper = upper_transfer.shape[1]
         any_spec = pl.BlockSpec(memory_space=pl.ANY)
-        smem = pl.BlockSpec(memory_space=pltpu.SMEM)
         dma = pltpu.SemaphoreType.DMA
+
+        def fixed(array):
+            return pltpu.with_memory_space_constraint(array, pltpu.HBM)
+
         return pl.pallas_call(
             functools.partial(kernel, branch_count, leaf_count),
             out_shape=jax.ShapeDtypeStruct(values.shape, F32),
-            in_specs=[any_spec] * 8 + [smem] * 2,
+            in_specs=[any_spec] * 10,
             out_specs=pl.BlockSpec(memory_space=pltpu.VMEM),
             scratch_shapes=[
+                pltpu.SMEM(coupling_source.shape, jnp.int32),
+                pltpu.SMEM(near_source.shape, jnp.int32),
                 pltpu.VMEM(values.shape, BF16),
                 pltpu.VMEM(leaf_basis.shape, BF16),
                 pltpu.VMEM(transfer.shape, BF16),
@@ -355,13 +401,15 @@
                 pltpu.VMEM(upper_transfer.shape[1:], BF16),
                 pltpu.VMEM((operators,) + upper_coupling.shape[2:], BF16),
                 pltpu.VMEM((operators,) + top_coupling.shape[2:], BF16),
-                pltpu.VMEM((3 * leaves, cols, leaf_size), BF16),
-                pltpu.VMEM((3 * rows, cols, rank), BF16),
-                pltpu.VMEM((upper + 1, cols, rank), BF16),
-                pltpu.VMEM((branch_count - 1, cols, rank), BF16),
+                pltpu.VMEM((3 * leaves, cols, 2 * leaf_size), BF16),
+                pltpu.VMEM((3 * rows, cols, 2 * rank), BF16),
+                pltpu.VMEM((leaf_count, rhs_count, operators * rank), BF16),
+                pltpu.VMEM((upper - leaf_count, cols, rank), BF16),
+                pltpu.VMEM((rhs_count, operators * rank), BF16),
+                pltpu.VMEM((branch_count - 1, rhs_count, operators * rank), BF16),
                 pltpu.VMEM((rows, rank, cols), F32),
                 pltpu.VMEM((leaves, leaf_size, cols), F32),
-                dma((8,)),
+                dma((10,)),
                 dma((4,)),
                 dma((4,)),
                 dma((leaf_count - 1,)),
@@ -370,19 +418,19 @@
                 dma((branch_count - 1,)),
             ],
             compiler_params=pltpu.CompilerParams(
-                collective_id=0, has_side_effects=True, vmem_limit_bytes=64 * 1024 * 1024
+                collective_id=0, has_side_effects=True, vmem_limit_bytes=32 * 1024 * 1024
             ),
         )(
-            values,
-            leaf_basis,
-            transfer,
-            local_coupling,
-            near_field,
-            upper_transfer,
-            upper_coupling,
-            top_coupling,
-            coupling_source,
-            near_source,
+            fixed(values),
+            fixed(leaf_basis),
+            fixed(transfer),
+            fixed(local_coupling),
+            fixed(near_field),
+            fixed(upper_transfer),
+            fixed(upper_coupling),
+            fixed(top_coupling),
+            fixed(coupling_source),
+            fixed(near_source),
         )
 
     in_specs = (

time: 24.1 us -> 17.5 us (0.73)
  Pallas kernels: 22.4 us -> 16.7 us
  local copies, waits for them, and re-layouts: 1.47 us -> 0.63 us
    pallas_call x1, Pallas kernels: 22.4 us -> 16.7 us  [per_device(): pl.pallas_call(functools.partial(kernel, branch_count, leaf_count), out_s...]
    unnamed x1, local copies, waits for them, and re-layouts: 1.47 us -> 0.63 us
where the time goes in v2:
time: 17.5 us; the launch traced here: 17.3 us
  Pallas kernels  16.7 us (95%)
  local copies, waits for them, and re-layouts  0.63 us (4%)
    pallas_call x1, Pallas kernels, per_device(): pl.pallas_call(functools.partial(kernel, branch_count, leaf_count), out_s...  16.7 us
    unnamed x1, local copies, waits for them, and re-layouts  0.63 us

profile of v2, /device:TPU:0, one launch (start us, length us, event | category | flops | bytes accessed | tf_op | source)
XLA Modules:
  0.0 17.3 jit_solution(15970461934758431920)
XLA Ops:
  0.0 16.7 %shard_map.100 = f32[2,16,512]{2,1,0:T(8,128)S(1)} custom-call(bf16[2,16,512]{2,1,0:T(8,128)(2,1)} %values.1, bf16[8,64,64]{2,1,0:T(8,128)(2,1)} %leaf_basis.1, bf16[14,64,64]{2,1,0:T(8,128)(2,1)} %transfer.1, bf16[2,14,12,64,64]{4,3,2,1,0:T(8,128)(2,1)} %local_coupling.1, bf16[2,8,12,64,64]{4,3,2,1,0:T(8,128)(2,1)} %near_field.1, ...), custom_call_target="tpu_custom_call" | custom-call | tf_op jit(solution)/shard_map/pallas_call | solution.py:388
  16.7 0.6 %copy.12 = f32[2,16,512]{2,1,0:T(8,128)} copy(f32[2,16,512]{2,1,0:T(8,128)S(1)} %shard_map.100) | data formatting | bytes 131072

commit v3 on v2

--- a/solution.py
+++ b/solution.py
@@ -96,19 +96,20 @@
         (leaf_basis, basis),
         (transfer, trans),
         (upper_transfer.at[0], up_trans),
+        (near_source, near_index),
+        (coupling_source, coupling_index),
         (near_field, near),
         (local_coupling, couple),
         (upper_coupling.at[:, 0], up_couple),
         (top_coupling.at[:, 0], top),
-        (near_source, near_index),
-        (coupling_source, coupling_index),
     ]
     loads = [
         pltpu.make_async_copy(src, dst, load_sem.at[i]) for i, (src, dst) in enumerate(pieces)
     ]
     for load in loads:
         load.start()
-    val_load, basis_load, trans_load, ut_load, near_load, couple_load, uc_load, top_load, ni_load, ci_load = loads
+    val_load, basis_load, trans_load, ut_load, ni_load, ci_load = loads[:6]
+    near_load, couple_load, uc_load, top_load = loads[6:]
 
     barrier = pltpu.get_barrier_semaphore()
 
@@ -143,12 +144,46 @@
         coef_win[2 * coef_pairs : 3 * coef_pairs] = jnp.zeros((coef_pairs, cols, 2 * rank), BF16)
 
     val_load.wait()
+    cells = val[...].reshape(cols, leaves * leaf_size)
+    for t in range(cell_pairs):
+        value_win[cell_pairs + t] = cells[:, 2 * t * leaf_size : 2 * (t + 1) * leaf_size]
+
+    greeted = leaf_count - 1 + branch_count - 1
+    greeted += low_edge.astype(jnp.int32) + high_edge.astype(jnp.int32)
+    pl.semaphore_wait(barrier, greeted)
+
+    def halo(window, size, kind, way):
+        place = 0 if way == 0 else 2 * size
+        other = p + 1 if way == 0 else p - 1
+        return pltpu.make_async_remote_copy(
+            src_ref=window.at[pl.ds(size, size)],
+            dst_ref=window.at[pl.ds(place, size)],
+            send_sem=halo_send.at[2 * kind + way],
+            recv_sem=halo_recv.at[2 * kind + way],
+            device_id=(other // leaf_count, lax.rem(other, leaf_count)),
+            device_id_type=MESH,
+        )
+
+    def for_ways(act):
+        @pl.when(p < last)
+        def _():
+            act(0)
+
+        @pl.when(p > 0)
+        def _():
+            act(1)
+
+    def value_halo(way):
+        return halo(value_win, cell_pairs, 0, way)
+
+    def coef_halo(way):
+        return halo(coef_win, coef_pairs, 1, way)
+
+    for_ways(lambda way: value_halo(way).start())
     basis_load.wait()
-    cells = val[...].reshape(cols, leaves * leaf_size)
     level = []
     for t in range(cell_pairs):
         pair = cells[:, 2 * t * leaf_size : 2 * (t + 1) * leaf_size]
-        value_win[cell_pairs + t] = pair
         level.append(dot(pair[:, :leaf_size], basis[2 * t]).astype(BF16))
         level.append(dot(pair[:, leaf_size:], basis[2 * t + 1]).astype(BF16))
     trans_load.wait()
@@ -163,10 +198,6 @@
         level = above
     leaf_roots[j] = dense(level[0])
 
-    greeted = leaf_count - 1 + branch_count - 1
-    greeted += low_edge.astype(jnp.int32) + high_edge.astype(jnp.int32)
-    pl.semaphore_wait(barrier, greeted)
-
     def leaf_copy(d, slot):
         return pltpu.make_async_remote_copy(
             src_ref=leaf_roots.at[slot],
@@ -180,29 +211,44 @@
     for d in range(1, leaf_count):
         leaf_copy(d, j).start()
 
-    def halo(window, size, kind, way):
-        place = 0 if way == 0 else 2 * size
-        other = p + 1 if way == 0 else p - 1
-        return pltpu.make_async_remote_copy(
-            src_ref=window.at[pl.ds(size, size)],
-            dst_ref=window.at[pl.ds(place, size)],
-            send_sem=halo_send.at[2 * kind + way],
-            recv_sem=halo_recv.at[2 * kind + way],
-            device_id=(other // leaf_count, lax.rem(other, leaf_count)),
-            device_id_type=MESH,
-        )
-
-    halos = ((value_win, cell_pairs, 0), (coef_win, coef_pairs, 1))
-
-    @pl.when(p < last)
-    def _():
-        for args in halos:
-            halo(*args, 0).start()
-
-    @pl.when(p > 0)
-    def _():
-        for args in halos:
-            halo(*args, 1).start()
+    for_ways(lambda way: coef_halo(way).start())
+
+    first = lax.broadcasted_iota(jnp.int32, (rank, cols), 1) < rhs_count
+
+    def pick(both):
+        return jnp.where(first, both[:rank], both[rank:])
+
+    def turn(window, size):
+        for m in range(3 * size):
+            pair = window[m]
+            half = pair.shape[1] // 2
+            window[3 * size + m] = jnp.concatenate([pair[:, half:], pair[:, :half]], axis=1)
+
+    def listed(matrices, row, count, window, source):
+        wide = side_by_side(
+            [matrices[:, row, m].reshape(operators * rank, rank) for m in range(count)]
+        )
+        picked = []
+        for m in range(0, count, 2):
+            half = window.shape[2] // 2
+            left, right = window[source(m)], window[source(m + 1)]
+            picked.append(jnp.concatenate([left[:, :half], right[:, half:]], axis=1))
+        return pick(dot_nt(wide, jnp.concatenate(picked, axis=1)))
+
+    for_ways(lambda way: value_halo(1 - way).wait_recv())
+    turn(value_win, cell_pairs)
+    ni_load.wait()
+    near_load.wait()
+
+    def near_step(t, carry):
+        def source(m):
+            s = near_index[t, m]
+            return jnp.bitwise_and(s + m, 1) * 3 * cell_pairs + jnp.right_shift(s, 1)
+
+        near_part[t] = listed(near, t, near_blocks, value_win, source)
+        return carry
+
+    lax.fori_loop(0, leaves, near_step, 0, unroll=4)
 
     ut_load.wait()
     for d in range(1, leaf_count):
@@ -235,51 +281,8 @@
     for d in range(1, branch_count):
         branch_copy(d).start()
 
-    first = lax.broadcasted_iota(jnp.int32, (rank, cols), 1) < rhs_count
-
-    def pick(both):
-        return jnp.where(first, both[:rank], both[rank:])
-
-    near_load.wait()
-
-    @pl.when(p > 0)
-    def _():
-        for args in halos:
-            halo(*args, 0).wait_recv()
-
-    @pl.when(p < last)
-    def _():
-        for args in halos:
-            halo(*args, 1).wait_recv()
-
-    for window, size, _ in halos:
-        for m in range(3 * size):
-            pair = window[m]
-            half = pair.shape[1] // 2
-            window[3 * size + m] = jnp.concatenate([pair[:, half:], pair[:, :half]], axis=1)
-
-    def listed(matrices, row, count, window, source):
-        wide = side_by_side(
-            [matrices[:, row, m].reshape(operators * rank, rank) for m in range(count)]
-        )
-        picked = []
-        for m in range(0, count, 2):
-            half = window.shape[2] // 2
-            left, right = window[source(m)], window[source(m + 1)]
-            picked.append(jnp.concatenate([left[:, :half], right[:, half:]], axis=1))
-        return pick(dot_nt(wide, jnp.concatenate(picked, axis=1)))
-
-    ni_load.wait()
-
-    def near_step(t, carry):
-        def source(m):
-            s = near_index[t, m]
-            return jnp.bitwise_and(s + m, 1) * 3 * cell_pairs + jnp.right_shift(s, 1)
-
-        near_part[t] = listed(near, t, near_blocks, value_win, source)
-        return carry
-
-    lax.fori_loop(0, leaves, near_step, 0, unroll=2)
+    for_ways(lambda way: coef_halo(1 - way).wait_recv())
+    turn(coef_win, coef_pairs)
     couple_load.wait()
     ci_load.wait()
 
@@ -300,7 +303,11 @@
             coupled[row] = listed(couple, row, blocks, coef_win, source)
             return carry
 
-        lax.fori_loop(0, count, couple_step, 0, unroll=2)
+        if step == 0:
+            lax.fori_loop(0, count, couple_step, 0, unroll=4)
+        else:
+            for t in range(count):
+                couple_step(t, 0)
 
     uc_load.wait()
     top_load.wait()
@@ -347,15 +354,8 @@
     for d in range(1, branch_count):
         branch_copy(d).wait_send()
 
-    @pl.when(p < last)
-    def _():
-        for args in halos:
-            halo(*args, 0).wait_send()
-
-    @pl.when(p > 0)
-    def _():
-        for args in halos:
-            halo(*args, 1).wait_send()
+    for_ways(lambda way: value_halo(way).wait_send())
+    for_ways(lambda way: coef_halo(way).wait_send())
 
 
 def solution(mesh):

time: 17.5 us -> 16.5 us (0.943)
  Pallas kernels: 16.7 us -> 15.7 us
    pallas_call x1, Pallas kernels: 16.7 us -> 15.7 us  [per_device(): pl.pallas_call(functools.partial(kernel, branch_count, leaf_count), out_s...]
where the time goes in v3:
time: 16.5 us; the launch traced here: 16.4 us
  Pallas kernels  15.7 us (95%)
  local copies, waits for them, and re-layouts  0.63 us (4%)
    pallas_call x1, Pallas kernels, per_device(): pl.pallas_call(functools.partial(kernel, branch_count, leaf_count), out_s...  15.7 us
    unnamed x1, local copies, waits for them, and re-layouts  0.63 us

profile of v3, /device:TPU:0, one launch (start us, length us, event | category | flops | bytes accessed | tf_op | source)
XLA Modules:
  0.0 16.4 jit_solution(6538562826834554700)
XLA Ops:
  0.0 15.7 %shard_map.100 = f32[2,16,512]{2,1,0:T(8,128)S(1)} custom-call(bf16[2,16,512]{2,1,0:T(8,128)(2,1)} %values.1, bf16[8,64,64]{2,1,0:T(8,128)(2,1)} %leaf_basis.1, bf16[14,64,64]{2,1,0:T(8,128)(2,1)} %transfer.1, bf16[2,14,12,64,64]{4,3,2,1,0:T(8,128)(2,1)} %local_coupling.1, bf16[2,8,12,64,64]{4,3,2,1,0:T(8,128)(2,1)} %near_field.1, ...), custom_call_target="tpu_custom_call" | custom-call | tf_op jit(solution)/shard_map/pallas_call | solution.py:388
  15.7 0.6 %copy.12 = f32[2,16,512]{2,1,0:T(8,128)} copy(f32[2,16,512]{2,1,0:T(8,128)S(1)} %shard_map.100) | data formatting | bytes 131072

commit v4 on v3

--- a/solution.py
+++ b/solution.py
@@ -91,6 +91,8 @@
     def undense(coef):
         return jnp.concatenate([coef[:, :rank], coef[:, rank:]], axis=0)
 
+    half = leaves // 2
+    chunks = [(0, half), (half, leaves)]
     pieces = [
         (values, val),
         (leaf_basis, basis),
@@ -98,18 +100,27 @@
         (upper_transfer.at[0], up_trans),
         (near_source, near_index),
         (coupling_source, coupling_index),
-        (near_field, near),
-        (local_coupling, couple),
-        (upper_coupling.at[:, 0], up_couple),
-        (top_coupling.at[:, 0], top),
     ]
+    for low, high in chunks:
+        for g in range(operators):
+            part = pl.ds(low, high - low)
+            pieces.append((near_field.at[g, part], near.at[g, part]))
+    pieces.append((upper_coupling.at[:, 0], up_couple))
+    pieces.append((top_coupling.at[:, 0], top))
+    chunks.append((leaves, rows))
+    for low, high in chunks:
+        for g in range(operators):
+            part = pl.ds(low, high - low)
+            pieces.append((local_coupling.at[g, part], couple.at[g, part]))
     loads = [
         pltpu.make_async_copy(src, dst, load_sem.at[i]) for i, (src, dst) in enumerate(pieces)
     ]
     for load in loads:
         load.start()
     val_load, basis_load, trans_load, ut_load, ni_load, ci_load = loads[:6]
-    near_load, couple_load, uc_load, top_load = loads[6:]
+    near_loads = loads[6 : 6 + 2 * operators]
+    uc_load, top_load = loads[6 + 2 * operators : 8 + 2 * operators]
+    couple_loads = loads[8 + 2 * operators :]
 
     barrier = pltpu.get_barrier_semaphore()
 
@@ -238,7 +249,6 @@
     for_ways(lambda way: value_halo(1 - way).wait_recv())
     turn(value_win, cell_pairs)
     ni_load.wait()
-    near_load.wait()
 
     def near_step(t, carry):
         def source(m):
@@ -248,7 +258,11 @@
         near_part[t] = listed(near, t, near_blocks, value_win, source)
         return carry
 
-    lax.fori_loop(0, leaves, near_step, 0, unroll=4)
+    for i, (low, high) in enumerate(chunks[:2]):
+        for load in near_loads[i * operators : (i + 1) * operators]:
+            load.wait()
+        for t in range(low, high):
+            near_step(t, 0)
 
     ut_load.wait()
     for d in range(1, leaf_count):
@@ -281,34 +295,6 @@
     for d in range(1, branch_count):
         branch_copy(d).start()
 
-    for_ways(lambda way: coef_halo(1 - way).wait_recv())
-    turn(coef_win, coef_pairs)
-    couple_load.wait()
-    ci_load.wait()
-
-    for step in range(LOG_LEAF):
-        count = leaves >> step
-        begin = starts[step]
-
-        def couple_step(t, carry, count=count, begin=begin, shift=LOG_LEAF - step):
-            row = begin + t
-
-            def source(m):
-                s = coupling_index[row, m]
-                side = jnp.right_shift(s, shift)
-                place = jnp.right_shift(jnp.bitwise_and(s, count - 1), 1)
-                turned = jnp.bitwise_and(s + m, 1) * 3 * coef_pairs
-                return turned + side * coef_pairs + begin // 2 + place
-
-            coupled[row] = listed(couple, row, blocks, coef_win, source)
-            return carry
-
-        if step == 0:
-            lax.fori_loop(0, count, couple_step, 0, unroll=4)
-        else:
-            for t in range(count):
-                couple_step(t, 0)
-
     uc_load.wait()
     top_load.wait()
     sides = []
@@ -321,6 +307,34 @@
         else:
             sibling = upper[offsets[step] - leaf_count + sibling]
         sides.append(pick(dot_nt(mats, sibling)))
+
+    for_ways(lambda way: coef_halo(1 - way).wait_recv())
+    turn(coef_win, coef_pairs)
+    ci_load.wait()
+
+    for step in range(LOG_LEAF):
+        count = leaves >> step
+        begin = starts[step]
+
+        def couple_step(t, carry, count=count, begin=begin, shift=LOG_LEAF - step):
+            row = begin + t
+
+            def source(m):
+                s = coupling_index[row, m]
+                side = jnp.right_shift(s, shift)
+                place = jnp.right_shift(jnp.bitwise_and(s, count - 1), 1)
+                turned = jnp.bitwise_and(s + m, 1) * 3 * coef_pairs
+                return turned + side * coef_pairs + begin // 2 + place
+
+            coupled[row] = listed(couple, row, blocks, coef_win, source)
+            return carry
+
+        for t in range(count):
+            for i, (low, _) in enumerate(chunks):
+                if begin + t == low:
+                    for load in couple_loads[i * operators : (i + 1) * operators]:
+                        load.wait()
+            couple_step(t, 0)
 
     for d in range(1, branch_count):
         branch_copy(d).wait_recv()
@@ -409,7 +423,7 @@
                 pltpu.VMEM((branch_count - 1, rhs_count, operators * rank), BF16),
                 pltpu.VMEM((rows, rank, cols), F32),
                 pltpu.VMEM((leaves, leaf_size, cols), F32),
-                dma((10,)),
+                dma((8 + 5 * operators,)),
                 dma((4,)),
                 dma((4,)),
                 dma((leaf_count - 1,)),

time: 16.5 us -> 16.6 us (level)
  no operation moved by 1% of the time
where the time goes in v4:
time: 16.6 us; the launch traced here: 16.4 us
  Pallas kernels  15.8 us (95%)
  local copies, waits for them, and re-layouts  0.63 us (4%)
    pallas_call x1, Pallas kernels, per_device(): pl.pallas_call(functools.partial(kernel, branch_count, leaf_count), out_s...  15.8 us
    unnamed x1, local copies, waits for them, and re-layouts  0.63 us

profile of v4, /device:TPU:0, one launch (start us, length us, event | category | flops | bytes accessed | tf_op | source)
XLA Modules:
  0.0 16.4 jit_solution(12337522616353809404)
XLA Ops:
  0.0 15.8 %shard_map.100 = f32[2,16,512]{2,1,0:T(8,128)S(1)} custom-call(bf16[2,16,512]{2,1,0:T(8,128)(2,1)} %values.1, bf16[8,64,64]{2,1,0:T(8,128)(2,1)} %leaf_basis.1, bf16[14,64,64]{2,1,0:T(8,128)(2,1)} %transfer.1, bf16[2,14,12,64,64]{4,3,2,1,0:T(8,128)(2,1)} %local_coupling.1, bf16[2,8,12,64,64]{4,3,2,1,0:T(8,128)(2,1)} %near_field.1, ...), custom_call_target="tpu_custom_call" | custom-call | tf_op jit(solution)/shard_map/pallas_call | solution.py:402
  15.8 0.6 %copy.12 = f32[2,16,512]{2,1,0:T(8,128)} copy(f32[2,16,512]{2,1,0:T(8,128)S(1)} %shard_map.100) | data formatting | bytes 131072

commit v5 on v4

--- a/solution.py
+++ b/solution.py
@@ -57,10 +57,10 @@
     value_win,
     coef_win,
     leaf_roots,
+    paths,
     upper,
     own_root,
     roots,
-    coupled,
     near_part,
     load_sem,
     halo_send,
@@ -107,15 +107,14 @@
             pieces.append((near_field.at[g, part], near.at[g, part]))
     pieces.append((upper_coupling.at[:, 0], up_couple))
     pieces.append((top_coupling.at[:, 0], top))
-    chunks.append((leaves, rows))
-    for low, high in chunks:
+    for low, high in ((leaves, rows), (0, leaves)):
         for g in range(operators):
             part = pl.ds(low, high - low)
             pieces.append((local_coupling.at[g, part], couple.at[g, part]))
     loads = [
         pltpu.make_async_copy(src, dst, load_sem.at[i]) for i, (src, dst) in enumerate(pieces)
     ]
-    for load in loads:
+    for load in loads[:3]:
         load.start()
     val_load, basis_load, trans_load, ut_load, ni_load, ci_load = loads[:6]
     near_loads = loads[6 : 6 + 2 * operators]
@@ -141,6 +140,9 @@
     @pl.when(high_edge)
     def _():
         greet(b + 1, 0)
+
+    for load in loads[3:]:
+        load.start()
 
     @pl.when(p == 0)
     def _():
@@ -246,6 +248,20 @@
             picked.append(jnp.concatenate([left[:, :half], right[:, half:]], axis=1))
         return pick(dot_nt(wide, jnp.concatenate(picked, axis=1)))
 
+    ut_load.wait()
+    offsets = [2 * leaf_count - 2 * (leaf_count >> step) for step in range(depth + 1)]
+    above = [up_trans[offsets[depth] - 2], up_trans[offsets[depth] - 1]]
+    for step in range(depth - 2, -1, -1):
+        below = []
+        for t, path in enumerate(above):
+            low = offsets[step] + 2 * t
+            mats = up_trans[low : low + 2].reshape(2 * rank, rank)
+            both = dot(mats, path).astype(BF16)
+            below += [both[:rank], both[rank:]]
+        above = below
+    for t, path in enumerate(above):
+        paths[t] = path
+
     for_ways(lambda way: value_halo(1 - way).wait_recv())
     turn(value_win, cell_pairs)
     ni_load.wait()
@@ -258,29 +274,17 @@
         near_part[t] = listed(near, t, near_blocks, value_win, source)
         return carry
 
-    for i, (low, high) in enumerate(chunks[:2]):
+    for i, (low, high) in enumerate(chunks):
         for load in near_loads[i * operators : (i + 1) * operators]:
             load.wait()
         for t in range(low, high):
             near_step(t, 0)
 
-    ut_load.wait()
     for d in range(1, leaf_count):
         leaf_copy(d, lax.rem(j + leaf_count - d, leaf_count)).wait_recv()
-    offsets = [2 * leaf_count - 2 * (leaf_count >> step) for step in range(depth + 1)]
     level = [undense(leaf_roots[m]) for m in range(leaf_count)]
-    for step in range(depth):
-        above = []
-        for t in range(leaf_count >> step + 1):
-            low = offsets[step] + 2 * t
-            pair = side_by_side(level[2 * t : 2 * t + 2])
-            mats = up_trans[low : low + 2].reshape(2 * rank, rank)
-            coef = dot(pair, mats).astype(BF16)
-            if step < depth - 1:
-                upper[offsets[step + 1] - leaf_count + t] = coef
-            above.append(coef)
-        level = above
-    own_root[...] = dense(level[0])
+    root = dot(side_by_side(level), paths[...].reshape(leaf_count * rank, rank))
+    own_root[...] = dense(root.astype(BF16))
 
     def branch_copy(d):
         return pltpu.make_async_remote_copy(
@@ -294,6 +298,17 @@
 
     for d in range(1, branch_count):
         branch_copy(d).start()
+
+    for step in range(depth - 1):
+        above = []
+        for t in range(leaf_count >> step + 1):
+            low = offsets[step] + 2 * t
+            pair = side_by_side(level[2 * t : 2 * t + 2])
+            mats = up_trans[low : low + 2].reshape(2 * rank, rank)
+            coef = dot(pair, mats).astype(BF16)
+            upper[offsets[step + 1] - leaf_count + t] = coef
+            above.append(coef)
+        level = above
 
     uc_load.wait()
     top_load.wait()
@@ -312,54 +327,64 @@
     turn(coef_win, coef_pairs)
     ci_load.wait()
 
-    for step in range(LOG_LEAF):
-        count = leaves >> step
-        begin = starts[step]
-
-        def couple_step(t, carry, count=count, begin=begin, shift=LOG_LEAF - step):
-            row = begin + t
-
-            def source(m):
-                s = coupling_index[row, m]
-                side = jnp.right_shift(s, shift)
-                place = jnp.right_shift(jnp.bitwise_and(s, count - 1), 1)
-                turned = jnp.bitwise_and(s + m, 1) * 3 * coef_pairs
-                return turned + side * coef_pairs + begin // 2 + place
-
-            coupled[row] = listed(couple, row, blocks, coef_win, source)
-            return carry
-
-        for t in range(count):
-            for i, (low, _) in enumerate(chunks):
-                if begin + t == low:
-                    for load in couple_loads[i * operators : (i + 1) * operators]:
-                        load.wait()
-            couple_step(t, 0)
-
-    for d in range(1, branch_count):
-        branch_copy(d).wait_recv()
-    tops = side_by_side(
-        [top[:, m].reshape(operators * rank, rank) for m in range(branch_count - 1)]
-    )
-    others = side_by_side([undense(roots[m]) for m in range(branch_count - 1)])
-    down = pick(dot_nt(tops, others)).astype(BF16)
-    for step in range(depth - 1, -1, -1):
+    rest = sides[depth - 1].astype(BF16)
+    for step in range(depth - 2, -1, -1):
         mat = up_trans[offsets[step] + jnp.right_shift(j, step)]
-        down = (sides[step] + dot(mat, down)).astype(BF16)
-    targets = [down]
+        rest = (sides[step] + dot(mat, rest)).astype(BF16)
+    targets = [jnp.concatenate([rest, paths[j]], axis=1)]
+    blank = jnp.zeros((2 * rank, rank), F32)
+
+    def couple_row(row, shift):
+        count = 1 << shift
+
+        def source(m):
+            s = coupling_index[row, m]
+            side = jnp.right_shift(s, shift)
+            place = jnp.right_shift(jnp.bitwise_and(s, count - 1), 1)
+            turned = jnp.bitwise_and(s + m, 1) * 3 * coef_pairs
+            return turned + side * coef_pairs + leaves - count + place
+
+        return listed(couple, row, blocks, coef_win, source)
+
+    known, from_top = [], []
     for step in range(LOG_LEAF - 1, -1, -1):
+        if step == LOG_LEAF - 1:
+            for load in couple_loads[:operators]:
+                load.wait()
+        if step == 0:
+            for load in couple_loads[operators:]:
+                load.wait()
         below = []
         for t, parent in enumerate(targets):
             low = starts[step] + 2 * t
             mats = trans[low : low + 2].reshape(2 * rank, rank)
-            both = coupled[low : low + 2].reshape(2 * rank, cols) + dot(mats, parent)
-            both = both.astype(BF16)
-            below += [both[:rank], both[rank:]]
+            pair = [couple_row(low + u, LOG_LEAF - step) for u in range(2)]
+            both = jnp.concatenate([jnp.concatenate(pair, axis=0), blank], axis=1)
+            both = (both + dot(mats, parent)).astype(BF16)
+            children = [both[:rank], both[rank:]]
+            below += children
+            if step == 0:
+                parts = []
+                for u in range(2):
+                    far = dot(basis[low + u], children[u])
+                    parts.append(near_part[low + u] + far[:, :cols])
+                    from_top.append(far[:, cols:].astype(BF16))
+                known.append(jnp.concatenate(parts, axis=0).T)
         targets = below
+    tops = side_by_side(
+        [top[:, m].reshape(operators * rank, rank) for m in range(branch_count - 1)]
+    )
+
+    for d in range(1, branch_count):
+        branch_copy(d).wait_recv()
+    others = side_by_side([undense(roots[m]) for m in range(branch_count - 1)])
+    crossed = dot_nt(others, tops)
+    down = jnp.concatenate([crossed[:rhs_count, :rank], crossed[rhs_count:, rank:]], axis=0)
+    down = down.astype(BF16)
     for t in range(0, leaves, 2):
-        parts = [near_part[u] + dot(basis[u], targets[u]) for u in (t, t + 1)]
-        turned = jnp.concatenate(parts, axis=0).T
-        out[:, :, t * leaf_size : (t + 2) * leaf_size] = turned.reshape(
+        mats = jnp.concatenate(from_top[t : t + 2], axis=0)
+        both = known[t // 2] + dot_nt(down, mats)
+        out[:, :, t * leaf_size : (t + 2) * leaf_size] = both.reshape(
             operators, rhs_count, 2 * leaf_size
         )
 
@@ -418,12 +443,12 @@
                 pltpu.VMEM((3 * leaves, cols, 2 * leaf_size), BF16),
                 pltpu.VMEM((3 * rows, cols, 2 * rank), BF16),
                 pltpu.VMEM((leaf_count, rhs_count, operators * rank), BF16),
+                pltpu.VMEM((leaf_count, rank, rank), BF16),
                 pltpu.VMEM((upper - leaf_count, cols, rank), BF16),
                 pltpu.VMEM((rhs_count, operators * rank), BF16),
                 pltpu.VMEM((branch_count - 1, rhs_count, operators * rank), BF16),
-                pltpu.VMEM((rows, rank, cols), F32),
                 pltpu.VMEM((leaves, leaf_size, cols), F32),
-                dma((8 + 5 * operators,)),
+                dma((8 + 4 * operators,)),
                 dma((4,)),
                 dma((4,)),
                 dma((leaf_count - 1,)),

time: 16.6 us -> 15.6 us (0.940)
  Pallas kernels: 15.8 us -> 14.8 us
    pallas_call x1, Pallas kernels: 15.8 us -> 14.8 us  [per_device(): pl.pallas_call(functools.partial(kernel, branch_count, leaf_count), out_s...]
where the time goes in v5:
time: 15.6 us; the launch traced here: 15.5 us
  Pallas kernels  14.8 us (95%)
  local copies, waits for them, and re-layouts  0.63 us (4%)
    pallas_call x1, Pallas kernels, per_device(): pl.pallas_call(functools.partial(kernel, branch_count, leaf_count), out_s...  14.8 us
    unnamed x1, local copies, waits for them, and re-layouts  0.63 us

profile of v5, /device:TPU:0, one launch (start us, length us, event | category | flops | bytes accessed | tf_op | source)
XLA Modules:
  0.0 15.5 jit_solution(6304245646925056692)
XLA Ops:
  0.0 14.8 %shard_map.100 = f32[2,16,512]{2,1,0:T(8,128)S(1)} custom-call(bf16[2,16,512]{2,1,0:T(8,128)(2,1)} %values.1, bf16[8,64,64]{2,1,0:T(8,128)(2,1)} %leaf_basis.1, bf16[14,64,64]{2,1,0:T(8,128)(2,1)} %transfer.1, bf16[2,14,12,64,64]{4,3,2,1,0:T(8,128)(2,1)} %local_coupling.1, bf16[2,8,12,64,64]{4,3,2,1,0:T(8,128)(2,1)} %near_field.1, ...), custom_call_target="tpu_custom_call" | custom-call | tf_op jit(solution)/shard_map/pallas_call | solution.py:427
  14.8 0.6 %copy.12 = f32[2,16,512]{2,1,0:T(8,128)} copy(f32[2,16,512]{2,1,0:T(8,128)S(1)} %shard_map.100) | data formatting | bytes 131072

commit v6 on v5

--- a/solution.py
+++ b/solution.py
@@ -56,6 +56,8 @@
     top,
     value_win,
     coef_win,
+    value_table,
+    coef_table,
     leaf_roots,
     paths,
     upper,
@@ -231,11 +233,25 @@
     def pick(both):
         return jnp.where(first, both[:rank], both[rank:])
 
-    def turn(window, size):
-        for m in range(3 * size):
-            pair = window[m]
-            half = pair.shape[1] // 2
-            window[3 * size + m] = jnp.concatenate([pair[:, half:], pair[:, :half]], axis=1)
+    def spread(pair, table, place):
+        half = pair.shape[1] // 2
+        turned = jnp.concatenate([pair[:, half:], pair[:, :half]], axis=1)
+        table[place] = jnp.concatenate([pair[:, :half], turned[:, half:]], axis=1)
+        table[place + 1] = jnp.concatenate([turned[:, :half], pair[:, half:]], axis=1)
+
+    def spread_values(side):
+        for t in range(0, leaves, 2):
+            spread(value_win[side * cell_pairs + t // 2], value_table, side * leaves + t)
+
+    def spread_coefs(side):
+        for step in range(LOG_LEAF):
+            count = leaves >> step
+            for t in range(0, count, 2):
+                pair = coef_win[side * coef_pairs + (starts[step] + t) // 2]
+                spread(pair, coef_table, 3 * starts[step] + side * count + t)
+
+    spread_values(1)
+    spread_coefs(1)
 
     def listed(matrices, row, count, window, source):
         wide = side_by_side(
@@ -263,15 +279,12 @@
         paths[t] = path
 
     for_ways(lambda way: value_halo(1 - way).wait_recv())
-    turn(value_win, cell_pairs)
+    spread_values(0)
+    spread_values(2)
     ni_load.wait()
 
     def near_step(t, carry):
-        def source(m):
-            s = near_index[t, m]
-            return jnp.bitwise_and(s + m, 1) * 3 * cell_pairs + jnp.right_shift(s, 1)
-
-        near_part[t] = listed(near, t, near_blocks, value_win, source)
+        near_part[t] = listed(near, t, near_blocks, value_table, lambda m: near_index[t, m])
         return carry
 
     for i, (low, high) in enumerate(chunks):
@@ -279,6 +292,23 @@
             load.wait()
         for t in range(low, high):
             near_step(t, 0)
+
+    for_ways(lambda way: coef_halo(1 - way).wait_recv())
+    spread_coefs(0)
+    spread_coefs(2)
+    ci_load.wait()
+
+    def couple_row(row, begin):
+        return listed(
+            couple, row, blocks, coef_table, lambda m: 3 * begin + coupling_index[row, m]
+        )
+
+    for load in couple_loads[:operators]:
+        load.wait()
+    ready = {}
+    for step in range(1, LOG_LEAF):
+        for row in range(starts[step], starts[step] + (leaves >> step)):
+            ready[row] = couple_row(row, starts[step])
 
     for d in range(1, leaf_count):
         leaf_copy(d, lax.rem(j + leaf_count - d, leaf_count)).wait_recv()
@@ -312,6 +342,8 @@
 
     uc_load.wait()
     top_load.wait()
+    for load in couple_loads[operators:]:
+        load.wait()
     sides = []
     for step in range(depth):
         own = jnp.right_shift(j, step)
@@ -323,10 +355,6 @@
             sibling = upper[offsets[step] - leaf_count + sibling]
         sides.append(pick(dot_nt(mats, sibling)))
 
-    for_ways(lambda way: coef_halo(1 - way).wait_recv())
-    turn(coef_win, coef_pairs)
-    ci_load.wait()
-
     rest = sides[depth - 1].astype(BF16)
     for step in range(depth - 2, -1, -1):
         mat = up_trans[offsets[step] + jnp.right_shift(j, step)]
@@ -334,31 +362,16 @@
     targets = [jnp.concatenate([rest, paths[j]], axis=1)]
     blank = jnp.zeros((2 * rank, rank), F32)
 
-    def couple_row(row, shift):
-        count = 1 << shift
-
-        def source(m):
-            s = coupling_index[row, m]
-            side = jnp.right_shift(s, shift)
-            place = jnp.right_shift(jnp.bitwise_and(s, count - 1), 1)
-            turned = jnp.bitwise_and(s + m, 1) * 3 * coef_pairs
-            return turned + side * coef_pairs + leaves - count + place
-
-        return listed(couple, row, blocks, coef_win, source)
-
     known, from_top = [], []
     for step in range(LOG_LEAF - 1, -1, -1):
-        if step == LOG_LEAF - 1:
-            for load in couple_loads[:operators]:
-                load.wait()
-        if step == 0:
-            for load in couple_loads[operators:]:
-                load.wait()
         below = []
         for t, parent in enumerate(targets):
             low = starts[step] + 2 * t
             mats = trans[low : low + 2].reshape(2 * rank, rank)
-            pair = [couple_row(low + u, LOG_LEAF - step) for u in range(2)]
+            if step == 0:
+                pair = [couple_row(low + u, starts[step]) for u in range(2)]
+            else:
+                pair = [ready[low + u] for u in range(2)]
             both = jnp.concatenate([jnp.concatenate(pair, axis=0), blank], axis=1)
             both = (both + dot(mats, parent)).astype(BF16)
             children = [both[:rank], both[rank:]]
@@ -440,6 +453,8 @@
                 pltpu.VMEM(upper_transfer.shape[1:], BF16),
                 pltpu.VMEM((operators,) + upper_coupling.shape[2:], BF16),
                 pltpu.VMEM((operators,) + top_coupling.shape[2:], BF16),
+                pltpu.VMEM((3 * leaves // 2, cols, 2 * leaf_size), BF16),
+                pltpu.VMEM((3 * rows // 2, cols, 2 * rank), BF16),
                 pltpu.VMEM((3 * leaves, cols, 2 * leaf_size), BF16),
                 pltpu.VMEM((3 * rows, cols, 2 * rank), BF16),
                 pltpu.VMEM((leaf_count, rhs_count, operators * rank), BF16),

time: 15.6 us -> 16.5 us (1.058)
  Pallas kernels: 14.8 us -> 15.8 us
    pallas_call x1, Pallas kernels: 14.8 us -> 15.8 us  [per_device(): pl.pallas_call(functools.partial(kernel, branch_count, leaf_count), out_s...]
where the time goes in v6:
time: 16.5 us; the launch traced here: 16.4 us
  Pallas kernels  15.8 us (96%)
  local copies, waits for them, and re-layouts  0.63 us (4%)
    pallas_call x1, Pallas kernels, per_device(): pl.pallas_call(functools.partial(kernel, branch_count, leaf_count), out_s...  15.8 us
    unnamed x1, local copies, waits for them, and re-layouts  0.63 us

profile of v6, /device:TPU:0, one launch (start us, length us, event | category | flops | bytes accessed | tf_op | source)
XLA Modules:
  0.0 16.4 jit_solution(7977498513235930314)
XLA Ops:
  0.0 15.8 %shard_map.100 = f32[2,16,512]{2,1,0:T(8,128)S(1)} custom-call(bf16[2,16,512]{2,1,0:T(8,128)(2,1)} %values.1, bf16[8,64,64]{2,1,0:T(8,128)(2,1)} %leaf_basis.1, bf16[14,64,64]{2,1,0:T(8,128)(2,1)} %transfer.1, bf16[2,14,12,64,64]{4,3,2,1,0:T(8,128)(2,1)} %local_coupling.1, bf16[2,8,12,64,64]{4,3,2,1,0:T(8,128)(2,1)} %near_field.1, ...), custom_call_target="tpu_custom_call" | custom-call | tf_op jit(solution)/shard_map/pallas_call | solution.py:440
  15.8 0.6 %copy.12 = f32[2,16,512]{2,1,0:T(8,128)} copy(f32[2,16,512]{2,1,0:T(8,128)S(1)} %shard_map.100) | data formatting | bytes 131072
